TPU v7x, 32 devices: a whole 2x2x4 slice. The times are simulated.
32 devices in a mesh: ctx: 16 (over z, y, x), fsdp: 2 (over core).
Axes of the slice: x: 2, y: 2, z: 4, core: 2. Of those that a mesh axis runs over, the one named last changes fastest.
Arguments:
- proj: bfloat16 [2, 2048, 12288], P('fsdp', 'ctx'), may hold values from -6 to 6
- short_taps: float32 [7, 12288], P(None, 'fsdp'), may hold values from -2 to 2
- long_filter: float32 [128, 256], P(None, 'fsdp'), may hold values from -0.5 to 0.5
- skip: float32 [4096], P('fsdp'), may hold values from -3 to 3
- grad_out: bfloat16 [2, 2048, 4096], P('fsdp', 'ctx'), may hold values from -6 to 6
- starts: int32 [2, 16, 4], P('fsdp', 'ctx'), may hold values from 0 to 128, as said below
Outputs:
- mixed_out: bfloat16 [2, 2048, 4096], P('fsdp', 'ctx')
- grad_proj: bfloat16 [2, 2048, 12288], P('fsdp', 'ctx')
- grad_short: float32 [7, 12288], P(None, 'fsdp')
- grad_long: float32 [128, 256], P(None, 'fsdp')
- grad_skip: float32 [4096], P('fsdp')
Inputs may be any that keep to these rules, and one draw needn't show every extreme that they name: Each list holds positions, within one device's 128 positions, at which documents start, increasing and without repeats; entries equal to 128 are empty and come after all others. Every window's first position starts a document.
All inputs are finite; a program needn't handle non-finite values.
Results may differ from a plain program's by a relative error of at most 0.007.
Values may be sent and summed in bfloat16 or wider, within the bound.
A program may use at most 128 MiB of HBM per device.

v0:
```python
import jax
import jax.numpy as jnp
from jax import lax
from jax.sharding import PartitionSpec as P

C = 4096
GROUP = 16
LEN = 128
SHORT = 7


far_back = 1 << 29


def prefix(value, axis, join, neutral):
    count, mine = (lax.axis_size(axis), lax.axis_index(axis))
    pieces = lax.all_gather(value, axis)
    so_far = jnp.full_like(value, 0) + jnp.asarray(neutral, value.dtype)

    def step(position, so_far):
        longer = join(so_far, pieces[position])
        return jnp.where(position < mine, longer, so_far)

    return lax.fori_loop(0, count - 1, step, so_far)


def passed_along(block, axis, distance):
    devices = range(lax.axis_size(axis))
    route = [(i - distance, i) for i in devices if i - distance in devices]
    return lax.ppermute(block, axis, route)


def toeplitz_tiles(values, rows_count, cols_count, low_diff):
    groups, taps_count = values.shape
    period = rows_count + cols_count + taps_count
    period_row = jnp.concatenate(
        [values, jnp.zeros((groups, period - taps_count), values.dtype)], axis=1
    )
    period_row = jnp.roll(period_row, low_diff, axis=1)
    repeated = jnp.tile(period_row, (1, rows_count))[:, : rows_count * (period - 1)]
    return repeated.reshape(groups, rows_count, period - 1)[:, :, :cols_count]


def lag_totals(product, rows_count, cols_count):
    groups = product.shape[0]
    flattened = product.reshape(groups, rows_count * cols_count)
    flattened = jnp.pad(flattened, ((0, 0), (0, rows_count)))
    totals = jnp.sum(flattened.reshape(groups, rows_count, cols_count + 1), axis=1)
    return totals[:, LEN:0:-1]


def body(proj, short_taps, long_filter, skip, grad_out, starts):
    taps_all, filt_all, skip_all = (
        lax.all_gather(short_taps, "fsdp", axis=1, tiled=True),
        lax.all_gather(long_filter, "fsdp", axis=1, tiled=True),
        lax.all_gather(skip, "fsdp", axis=0, tiled=True),
    )
    source = proj[0]
    tok_rows = source.shape[0]
    win_rows = tok_rows + LEN
    groups = C // GROUP
    block_groups = min(groups, 32)
    block_count = groups // block_groups
    positions = jnp.arange(tok_rows, dtype=jnp.int32)
    listed = starts[0, 0]
    usable = listed < tok_rows
    own_last = jnp.max(jnp.where(usable, listed, -far_back)).reshape(1)
    ctx_index = lax.axis_index("ctx")
    placed = jnp.where(own_last >= 0, own_last + ctx_index * tok_rows, -far_back)
    before = prefix(placed, "ctx", jnp.maximum, jnp.full((1,), -far_back, jnp.int32))
    prior_start = before[0] - ctx_index * tok_rows
    candidates = jnp.where(
        usable[None, :] & (listed[None, :] <= positions[:, None]), listed[None, :], -far_back
    )
    last_local = jnp.maximum(prior_start, jnp.max(candidates, axis=1))
    short_tail = passed_along(source[tok_rows - (SHORT - 1) :], "ctx", 1)
    padded = jnp.concatenate([short_tail, source], axis=0)
    linked_rows = [(last_local <= positions - offset)[:, None] for offset in range(SHORT)]
    earlier_rows = [
        padded[SHORT - 1 - offset : SHORT - 1 - offset + tok_rows] for offset in range(SHORT)
    ]
    featured = jnp.zeros((tok_rows, 3 * C), jnp.float32)
    for offset in range(SHORT):
        featured = featured + taps_all[offset] * jnp.where(
            linked_rows[offset], earlier_rows[offset].astype(jnp.float32), 0.0
        )
    query_feat = featured[:, :C]
    key_feat = featured[:, C : 2 * C]
    value_feat = featured[:, 2 * C :]
    gating = (key_feat * value_feat).astype(jnp.bfloat16)
    gate_tail = passed_along(gating[tok_rows - (LEN - 1) :], "ctx", 1)
    window = jnp.concatenate([jnp.zeros((1, C), jnp.bfloat16), gate_tail, gating], axis=0)
    window_cols = window.T.reshape(groups, GROUP, win_rows)
    window_mask = last_local[:, None] <= (jnp.arange(win_rows, dtype=jnp.int32) - LEN)[None, :]
    reversed_taps = filt_all[::-1].astype(jnp.bfloat16).T
    zero_half = jnp.zeros((), jnp.bfloat16)
    upstream = grad_out[0].astype(jnp.float32)
    through = upstream * query_feat
    grad_long_in = through.astype(jnp.bfloat16)
    grad_cols = grad_long_in.T.reshape(groups, GROUP, tok_rows)

    def group_block(matrix, block_id):
        return lax.dynamic_slice_in_dim(matrix, block_id * block_groups, block_groups, 0)

    def ahead_tiles(block_id):
        return jnp.where(
            window_mask[None],
            toeplitz_tiles(group_block(reversed_taps, block_id), tok_rows, win_rows, 1),
            zero_half,
        )

    def filter_block(rows_blk, win_blk):
        product = jnp.einsum("gct,gcs->gts", rows_blk, win_blk, preferred_element_type=jnp.float32)
        return lag_totals(jnp.where(window_mask[None], product, 0.0), tok_rows, win_rows)

    def joint_block(block_id, state):
        long_cols, spread_cols, lag_grid = state
        tiles = ahead_tiles(block_id)
        win_blk = group_block(window_cols, block_id)
        rows_blk = group_block(grad_cols, block_id)
        fwd_out = jnp.einsum("gcs,gts->gct", win_blk, tiles, preferred_element_type=jnp.float32)
        bwd_out = jnp.einsum("gct,gts->gcs", rows_blk, tiles, preferred_element_type=jnp.float32)
        start_row = block_id * block_groups
        long_cols = lax.dynamic_update_slice_in_dim(long_cols, fwd_out, start_row, 0)
        spread_cols = lax.dynamic_update_slice_in_dim(spread_cols, bwd_out, start_row, 0)
        lag_grid = lax.dynamic_update_slice_in_dim(
            lag_grid, filter_block(rows_blk, win_blk), start_row, 0
        )
        return (long_cols, spread_cols, lag_grid)

    long_cols, spread_cols, lag_grid = lax.fori_loop(
        0,
        block_count,
        joint_block,
        (
            jnp.zeros((groups, GROUP, tok_rows), jnp.float32),
            jnp.zeros((groups, GROUP, win_rows), jnp.float32),
            jnp.zeros((groups, LEN), jnp.float32),
        ),
    )
    spread = spread_cols.reshape(C, win_rows).T
    returned = passed_along(spread[1:LEN], "ctx", -1)
    grad_gate = spread[LEN:] + jnp.concatenate(
        [jnp.zeros((tok_rows - (LEN - 1), C), jnp.float32), returned], axis=0
    )
    long_out = long_cols.reshape(C, tok_rows).T
    gate_f = gating.astype(jnp.float32)
    combined = long_out + skip_all * gate_f
    mixed_out = (query_feat * combined).astype(jnp.bfloat16)
    grad_query = upstream * combined
    grad_gate = grad_gate + skip_all * through
    grad_feat = jnp.concatenate([grad_query, grad_gate * value_feat, grad_gate * key_feat], axis=1)
    spread_short = jnp.zeros((tok_rows + SHORT - 1, 3 * C), jnp.float32)
    for offset in range(SHORT):
        contrib = taps_all[offset] * jnp.where(linked_rows[offset], grad_feat, 0.0)
        spread_short = spread_short + jnp.pad(contrib, ((SHORT - 1 - offset, offset), (0, 0)))
    returned_short = passed_along(spread_short[: SHORT - 1], "ctx", -1)
    grad_source = spread_short[SHORT - 1 :] + jnp.concatenate(
        [jnp.zeros((tok_rows - (SHORT - 1), 3 * C), jnp.float32), returned_short], axis=0
    )
    short_parts = []
    for offset in range(SHORT):
        earlier = jnp.where(linked_rows[offset], earlier_rows[offset].astype(jnp.float32), 0.0)
        short_parts.append(jnp.sum(grad_feat * earlier, axis=0))
    scaling = float(lax.axis_size("fsdp") * lax.axis_size("ctx") * tok_rows) ** (-0.5)
    grad_terms = (
        jnp.stack(short_parts) * scaling,
        lag_grid.T * scaling,
        jnp.sum(through * gate_f, axis=0) * scaling,
    )
    summed = lax.psum((grad_terms[0], grad_terms[1], grad_terms[2]), "ctx")
    reduced = (
        lax.psum_scatter(summed[0], "fsdp", scatter_dimension=1, tiled=True),
        lax.psum_scatter(summed[1], "fsdp", scatter_dimension=1, tiled=True),
        lax.psum_scatter(summed[2], "fsdp", scatter_dimension=0, tiled=True),
    )
    return (
        mixed_out[None],
        grad_source.astype(jnp.bfloat16)[None],
        reduced[0],
        reduced[1],
        reduced[2],
    )


def solution(mesh):
    placed = (
        P("fsdp", "ctx", None),
        P(None, "fsdp"),
        P(None, "fsdp"),
        P("fsdp"),
        P("fsdp", "ctx", None),
        P("fsdp", "ctx", None),
    )
    return jax.shard_map(
        body,
        mesh=mesh,
        in_specs=placed,
        out_specs=(
            P("fsdp", "ctx", None),
            P("fsdp", "ctx", None),
            P(None, "fsdp"),
            P(None, "fsdp"),
            P("fsdp"),
        ),
        check_vma=False,
    )
```

profile of v0, /device:TPU:0, one launch (start us, length us, event | category | flops | bytes accessed | tf_op | source)
XLA Modules:
  0.0 764.8 jit_solution(3808949127715189536)
XLA Ops:
  22.5 14.1 %all-reduce.12 = s32[16]{0:T(128)S(1)} all-reduce(s32[16]{0:T(128)S(1)} %dynamic-update-slice), channel_id=1, replica_groups=mesh['ctx'=16,'fsdp'=2] {'ctx'}, use_global_device_ids=true, to_apply=%add.12 | all-reduce | flops 16 | bytes 128
  36.6 18.8 %while.33 = (s32[]{:T(128)}, s32[1]{0:T(128)}, s32[]{:T(128)}, s32[16,1]{0,1:T(1,128)S(1)}, s32[]{:T(128)}) while((s32[]{:T(128)}, s32[1]{0:T(128)}, s32[]{:T(128)}, s32[16,1]{0,1:T(1,128)S(1)}, s32[]{:T(128)}) %tuple.115), condition=%wide.region_2.3_spmd, body=%wide.region_1.2_spmd.sunk | while | flops 5 | bytes 107 | solution.py:24
  64.1 26.2 %multiply_add_fusion = f32[128,12288]{0,1:T(8,128)S(1)} fusion(bf16[128,12288]{0,1:T(8,128)(2,1)S(1)} %bitcast.85, f32[12288]{0:T(1024)S(1)} %bitcast.99, f32[12288]{0:T(1024)S(1)} %bitcast.101, f32[12288]{0:T(1024)S(1)} %bitcast.93, f32[12288]{0:T(1024)S(1)} %bitcast.103, f32[12288]{0:T(1024)S(1)} %bitcast.95, f32[12288]{0:T(1024)S(1)} %bitcast.105, ...), kind=kLoop, calls=%fused_computation.51 | loop fusion | flops 70778880 | bytes 9929600 | tf_op jit(solution)/shard_map/add | solution.py:84
  102.6 19.8 %collective-permute-done.1 = bf16[127,4096]{0,1:T(8,128)(2,1)} collective-permute-done((bf16[127,4096]{0,1:T(8,128)(2,1)}, bf16[127,4096]{0,1:T(8,128)(2,1)}, u32[]{:S(2)}, u32[]{:S(2)}) %collective-permute-start.1) | collective-permute-done | bytes 1040416 | tf_op jit(solution)/shard_map/ppermute | solution.py:30
  130.3 309.5 %while.34 = (s32[]{:T(128)}, f32[256,16,128]{2,1,0:T(8,128)}, f32[256,16,256]{2,1,0:T(8,128)}, f32[256,128]{1,0:T(8,128)S(1)}, bf16[256,16,256]{2,1,0:T(8,128)(2...) while((s32[]{:T(128)}, f32[256,16,128]{2,1,0:T(8,128)}, ...), condition=%wide.region_6.7_spmd.clone, body=%wide.region_4.6_spmd.clone.sunk | while | flops 104886240 | bytes 69139168 | solution.py:131
  135.6 9.6 %reshape.150 = bf16[32,128,511]{2,1,0:T(8,128)(2,1)} reshape(bf16[32,65408]{1,0:T(8,128)(2,1)} %slice.294) | data formatting | bytes 8372224 | tf_op jit(solution)/shard_map/while/body/eval_jaxpr/reshape | solution.py:41
  154.6 8.0 %reshape.151 = f32[32,128,257]{2,1,0:T(8,128)} reshape(f32[32,32896]{1,0:T(8,128)} %pad.248) | data formatting | bytes 8421376 | tf_op jit(solution)/shard_map/while/body/eval_jaxpr/reshape | solution.py:48
  174.3 9.6 %reshape.150 = bf16[32,128,511]{2,1,0:T(8,128)(2,1)} reshape(bf16[32,65408]{1,0:T(8,128)(2,1)} %slice.294) | data formatting | bytes 8372224 | tf_op jit(solution)/shard_map/while/body/eval_jaxpr/reshape | solution.py:41
  212.9 9.6 %reshape.150 = bf16[32,128,511]{2,1,0:T(8,128)(2,1)} reshape(bf16[32,65408]{1,0:T(8,128)(2,1)} %slice.294) | data formatting | bytes 8372224 | tf_op jit(solution)/shard_map/while/body/eval_jaxpr/reshape | solution.py:41
  232.0 8.0 %reshape.151 = f32[32,128,257]{2,1,0:T(8,128)} reshape(f32[32,32896]{1,0:T(8,128)} %pad.248) | data formatting | bytes 8421376 | tf_op jit(solution)/shard_map/while/body/eval_jaxpr/reshape | solution.py:48
  251.6 9.6 %reshape.150 = bf16[32,128,511]{2,1,0:T(8,128)(2,1)} reshape(bf16[32,65408]{1,0:T(8,128)(2,1)} %slice.294) | data formatting | bytes 8372224 | tf_op jit(solution)/shard_map/while/body/eval_jaxpr/reshape | solution.py:41
  290.3 9.6 %reshape.150 = bf16[32,128,511]{2,1,0:T(8,128)(2,1)} reshape(bf16[32,65408]{1,0:T(8,128)(2,1)} %slice.294) | data formatting | bytes 8372224 | tf_op jit(solution)/shard_map/while/body/eval_jaxpr/reshape | solution.py:41
  328.9 9.6 %reshape.150 = bf16[32,128,511]{2,1,0:T(8,128)(2,1)} reshape(bf16[32,65408]{1,0:T(8,128)(2,1)} %slice.294) | data formatting | bytes 8372224 | tf_op jit(solution)/shard_map/while/body/eval_jaxpr/reshape | solution.py:41
  367.6 9.6 %reshape.150 = bf16[32,128,511]{2,1,0:T(8,128)(2,1)} reshape(bf16[32,65408]{1,0:T(8,128)(2,1)} %slice.294) | data formatting | bytes 8372224 | tf_op jit(solution)/shard_map/while/body/eval_jaxpr/reshape | solution.py:41
  406.2 9.6 %reshape.150 = bf16[32,128,511]{2,1,0:T(8,128)(2,1)} reshape(bf16[32,65408]{1,0:T(8,128)(2,1)} %slice.294) | data formatting | bytes 8372224 | tf_op jit(solution)/shard_map/while/body/eval_jaxpr/reshape | solution.py:41
  447.3 45.8 %collective-permute-done.2 = f32[127,4096]{0,1:T(8,128)} collective-permute-done((f32[127,4096]{0,1:T(8,128)}, f32[127,4096]{0,1:T(8,128)}, u32[]{:S(2)}, u32[]{:S(2)}) %collective-permute-start.2) | collective-permute-done | bytes 2080800 | tf_op jit(solution)/shard_map/ppermute | solution.py:30
  501.9 18.0 %multiply_reduce_fusion = (f32[12288]{0:T(1024)S(1)}, f32[12288]{0:T(1024)S(1)}, f32[12288]{0:T(1024)}, f32[128,12288]{0,1:T(8,128)}) fusion(pred[128]{0:T(512)(128)(4,1)S(1)} %copy-done.32, bf16[128,12288]{0,1:T(8,128)(2,1)S(1)} %bitcast.86, bf16[6,12288]{0,1:T(8,128)(2,1)S(1)} %copy-done.2, f32[128,4096]{0,1:T(8,128)S(1)} %slice_multiply_fusion.1, ...), kind=kLoop, calls=%fused_computation.37 | loop fusion | flops 39284736 | bytes 16073088 | tf_op jit(solution)/shard_map/reduce_sum | solution.py:164
  520.0 14.5 %multiply_reduce_fusion.1 = (f32[12288]{0:T(1024)}, f32[12288]{0:T(1024)}, f32[12288]{0:T(1024)}, f32[128,12288]{0,1:T(8,128)}) fusion(pred[128]{0:T(512)(128)(4,1)S(1)} %copy-done.34, bf16[128,12288]{0,1:T(8,128)(2,1)S(1)} %bitcast.87, bf16[6,12288]{0,1:T(8,128)(2,1)S(1)} %copy-done.2, f32[128,4096]{0,1:T(8,128)S(1)} %slice_multiply_fusion.1, ...), kind=kLoop, calls=%fused_computation.38 | loop fusion | flops 39284736 | bytes 16073088 | tf_op jit(solution)/shard_map/reduce_sum | solution.py:164
  534.5 10.7 %multiply_reduce_fusion.6 = (f32[12288]{0:T(1024)S(1)}, f32[128,12288]{0,1:T(8,128)}, f32[128,12288]{0,1:T(8,128)}, f32[128,12288]{0,1:T(8,128)}) fusion(pred[128]{0:T(512)(128)(4,1)S(1)} %copy-done.41, bf16[1,128,12288]{1,2,0:T(8,128)(2,1)S(1)} %copy.33, f32[128,4096]{0,1:T(8,128)S(1)} %slice_multiply_fusion.1, f32[128,4096]{0,1:T(8,128)S(1)} %get-tuple-element.370, ...), kind=kLoop, calls=%fused_computation.43 | loop fusion | flops 18862080 | bytes 28508544 | tf_op jit(solution)/shard_map/reduce_sum | solution.py:164
  545.2 13.9 %select_multiply_fusion.4 = (f32[128,12288]{0,1:T(8,128)}, f32[128,12288]{0,1:T(8,128)}) fusion(f32[12288]{0:T(1024)S(1)} %bitcast.96, pred[128]{0:T(512)(128)(4,1)S(1)} %copy-done.30, f32[128,4096]{0,1:T(8,128)S(1)} %slice_multiply_fusion.1, f32[128,4096]{0,1:T(8,128)S(1)} %get-tuple-element.370, f32[128,4096]{0,1:T(8,128)S(1)} %get-tuple-element.384, ...), kind=kLoop, calls=%fused_computation.48 | loop fusion | flops 9437184 | bytes 18972928 | tf_op jit(solution)/shard_map/mul | solution.py:155
  560.6 25.2 %pad_add_fusion = f32[134,12288]{0,1:T(8,128)S(1)} fusion(f32[128,12288]{0,1:T(8,128)} %get-tuple-element.381, f32[128,12288]{0,1:T(8,128)} %get-tuple-element.380, f32[128,12288]{0,1:T(8,128)} %get-tuple-element.383, f32[128,12288]{0,1:T(8,128)} %get-tuple-element.376, f32[128,12288]{0,1:T(8,128)} %get-tuple-element.382, ...), kind=kLoop, calls=%fused_computation.23 | loop fusion | flops 9879552 | bytes 50626560 | tf_op jit(solution)/shard_map/add | solution.py:156
  603.6 43.2 %psum.26 = f32[2048]{0:T(1024)} all-reduce(f32[2048]{0:T(1024)S(1)} %dynamic-slice.2), channel_id=1, replica_groups=mesh['ctx'=16,'fsdp'=2] {'ctx'}, use_global_device_ids=true, to_apply=%region_19.20 | all-reduce | flops 2048 | bytes 16384 | tf_op jit(solution)/shard_map/psum | solution.py:171
  652.1 8.2 %fusion.18 = bf16[1,128,12288]{1,2,0:T(8,128)(2,1)S(1)} fusion(f32[6,12288]{0,1:T(8,128)} %copy.38, f32[134,12288]{0,1:T(8,128)} %copy-done.1), kind=kLoop, calls=%fused_computation.59 | loop fusion | flops 3145728 | bytes 9732096 | tf_op jit(solution)/shard_map/broadcast_in_dim | solution.py:179
  663.1 92.1 %all-reduce.17.cloned.1.call-done = (f32[7,6144]{1,0:T(8,128)}, f32[128,128]{1,0:T(8,128)}) async-done(((f32[7,6144]{1,0:T(8,128)}, f32[128,128]{1,0:T(8,128)}), (f32[7,6144]{1,0:T(8,128)}, f32[128,128]{1,0:T(8,128)})) %all-reduce.17.cloned.1.call-update) | async-done | bytes 237584 | tf_op jit(solution)/shard_map/psum | solution.py:171
  (311 shorter events, 313.4 us)
Async XLA Ops:
  7.2 53.0 %copy-start.42 = (s32[1,1,4]{2,1,0:T(1,128)S(1)}, s32[1,1,4]{2,1,0:T(1,128)}, u32[]{:S(2)}) copy-start(s32[1,1,4]{2,1,0:T(1,128)} %param.15) | copy-start | bytes 52
  7.2 48.3 %copy-start.18 = (f32[7,6144]{1,0:T(8,128)S(1)}, f32[7,6144]{1,0:T(8,128)}, u32[]{:S(2)}) copy-start(f32[7,6144]{1,0:T(8,128)} %param.11) | copy-start | bytes 516100
  7.2 644.9 %reduce-scatter.5.cloned.1.call-start = ((), (), s32[]{:S(2)}) async-start(), calls=%async_computation.3 | async-start | bytes 196608 | tf_op jit(solution)/shard_map/reduce_scatter | solution.py:174
  8.9 51.4 %collective-permute-start = (bf16[6,12288]{1,0:T(8,128)(2,1)}, bf16[6,12288]{1,0:T(8,128)(2,1)}, u32[]{:S(2)}, u32[]{:S(2)}) collective-permute-start(bf16[6,12288]{1,0:T(8,128)(2,1)} %slice_bitcast_fusion), channel_id=1, source_target_pairs={{0,2},{2,4},{4,6},{6,8},{8,10},{10,12},{12,14},{14,16},{16,18},{18... | collective-permute-start | bytes 442376 | tf_op jit(solution)/shard_map/ppermute | solution.py:30
  57.8 32.5 %copy-start.6 = (f32[1,12288]{1,0:T(1,128)}, f32[1,12288]{1,0:T(1,128)S(1)}, u32[]{:S(2)}) copy-start(f32[1,12288]{1,0:T(1,128)S(1)} %get-tuple-element.390) | copy-start | bytes 147460
  57.8 32.5 %copy-start.8 = (f32[1,12288]{1,0:T(1,128)}, f32[1,12288]{1,0:T(1,128)S(1)}, u32[]{:S(2)}) copy-start(f32[1,12288]{1,0:T(1,128)S(1)} %get-tuple-element.385) | copy-start | bytes 147460
  57.8 32.5 %copy-start.10 = (f32[1,12288]{1,0:T(1,128)}, f32[1,12288]{1,0:T(1,128)S(1)}, u32[]{:S(2)}) copy-start(f32[1,12288]{1,0:T(1,128)S(1)} %get-tuple-element.386) | copy-start | bytes 147460
  57.8 32.5 %copy-start.12 = (f32[1,12288]{1,0:T(1,128)}, f32[1,12288]{1,0:T(1,128)S(1)}, u32[]{:S(2)}) copy-start(f32[1,12288]{1,0:T(1,128)S(1)} %get-tuple-element.387) | copy-start | bytes 147460
  57.8 32.5 %copy-start.14 = (f32[1,12288]{1,0:T(1,128)}, f32[1,12288]{1,0:T(1,128)S(1)}, u32[]{:S(2)}) copy-start(f32[1,12288]{1,0:T(1,128)S(1)} %get-tuple-element.389) | copy-start | bytes 147460
  57.9 32.5 %copy-start.16 = (f32[1,12288]{1,0:T(1,128)}, f32[1,12288]{1,0:T(1,128)S(1)}, u32[]{:S(2)}) copy-start(f32[1,12288]{1,0:T(1,128)S(1)} %get-tuple-element.391) | copy-start | bytes 147460
  64.1 29.0 %copy-start.4 = (bf16[1,128,4096]{1,2,0:T(8,128)(2,1)S(1)}, bf16[1,128,4096]{1,2,0:T(8,128)(2,1)}, u32[]{:S(2)}) copy-start(bf16[1,128,4096]{1,2,0:T(8,128)(2,1)} %copy.36) | copy-start | bytes 3145732
  97.5 25.0 %collective-permute-start.1 = (bf16[127,4096]{0,1:T(8,128)(2,1)}, bf16[127,4096]{0,1:T(8,128)(2,1)}, u32[]{:S(2)}, u32[]{:S(2)}) collective-permute-start(bf16[127,4096]{0,1:T(8,128)(2,1)} %slice.171), channel_id=1, source_target_pairs={{0,2},{2,4},{4,6},{6,8},{8,10},{10,12},{12,14},{14,16},{16,18},{18... | collective-permute-start | bytes 3121160 | tf_op jit(solution)/shard_map/ppermute | solution.py:30
  130.3 314.4 %copy-start.35 = (f32[2048]{0:T(1024)S(1)}, f32[2048]{0:T(1024)}, u32[]{:S(2)}) copy-start(f32[2048]{0:T(1024)} %param.13) | copy-start | bytes 24580
  443.3 49.8 %collective-permute-start.2 = (f32[127,4096]{0,1:T(8,128)}, f32[127,4096]{0,1:T(8,128)}, u32[]{:S(2)}, u32[]{:S(2)}) collective-permute-start(f32[127,4096]{0,1:T(8,128)} %slice.173), channel_id=1, source_target_pairs={{2,0},{4,2},{6,4},{8,6},{10,8},{12,10},{14,12},{16,14},{18,16},{20... | collective-permute-start | bytes 6242312 | tf_op jit(solution)/shard_map/ppermute | solution.py:30
  447.3 204.8 %reduce-scatter.3.cloned.1.call-start = ((), (), s32[]{:S(2)}) async-start(), calls=%async_computation.2 | async-start | bytes 589824 | tf_op jit(solution)/shard_map/reduce_scatter | solution.py:173
  501.9 18.1 %copy-start.15 = (f32[1,12288]{1,0:T(1,128)S(1)}, f32[1,12288]{1,0:T(1,128)}, u32[]{:S(2)}) copy-start(f32[1,12288]{1,0:T(1,128)} %copy-done.14) | copy-start | bytes 147460
  501.9 18.1 %copy-start.28 = (pred[128]{0:T(512)(128)(4,1)S(1)}, pred[128]{0:T(512)(128)(4,1)}, u32[]{:S(2)}) copy-start(pred[128]{0:T(512)(128)(4,1)} %copy-done.27) | copy-start | bytes 388
  501.9 18.0 %copy-start.34 = (pred[128]{0:T(512)(128)(4,1)S(1)}, pred[128]{0:T(512)(128)(4,1)}, u32[]{:S(2)}) copy-start(pred[128]{0:T(512)(128)(4,1)} %copy-done.33) | copy-start | bytes 388
  501.9 18.0 %copy-start.37 = (pred[128]{0:T(512)(128)(4,1)S(1)}, pred[128]{0:T(512)(128)(4,1)}, u32[]{:S(2)}) copy-start(pred[128]{0:T(512)(128)(4,1)} %copy-done.36) | copy-start | bytes 388
  519.9 14.6 %copy-start.9 = (f32[1,12288]{1,0:T(1,128)S(1)}, f32[1,12288]{1,0:T(1,128)}, u32[]{:S(2)}) copy-start(f32[1,12288]{1,0:T(1,128)} %copy-done.8) | copy-start | bytes 147460
  519.9 14.5 %copy-start.11 = (f32[1,12288]{1,0:T(1,128)S(1)}, f32[1,12288]{1,0:T(1,128)}, u32[]{:S(2)}) copy-start(f32[1,12288]{1,0:T(1,128)} %copy-done.10) | copy-start | bytes 147460
  560.5 194.7 %all-reduce.17.cloned.1.call-start = ((), (), s32[]{:S(2)}) async-start(), calls=%async_computation.4 | async-start | bytes 524288 | tf_op jit(solution)/shard_map/psum | solution.py:171
  593.1 53.6 %copy-start.5 = (bf16[128,4096]{0,1:T(8,128)(2,1)S(1)}, bf16[128,4096]{0,1:T(8,128)(2,1)}, u32[]{:S(2)}) copy-start(bf16[128,4096]{0,1:T(8,128)(2,1)} %get-tuple-element.375) | copy-start | bytes 3145732
  597.6 50.4 %collective-permute-start.3 = (f32[6,12288]{1,0:T(8,128)S(1)}, f32[6,12288]{1,0:T(8,128)S(1)}, u32[]{:S(2)}, u32[]{:S(2)}) collective-permute-start(f32[6,12288]{1,0:T(8,128)S(1)} %copy.37), channel_id=1, source_target_pairs={{2,0},{4,2},{6,4},{8,6},{10,8},{12,10},{14,12},{16,14},{18,16},{20... | collective-permute-start | bytes 884744 | tf_op jit(solution)/shard_map/ppermute | solution.py:30
  (35 other events, 275.7 us)
Sparse Core Ops, SparseCore 0:
  447.4 10.8 reduce-scatter.4
  560.7 8.4 reduce-scatter.2
  652.2 102.9 all-reduce.16
where the time goes:
time: 768 us; the launch traced here: 765 us
  local copies, waits for them, and re-layouts  280 us (36%)
  other arithmetic  161 us (21%)
  waiting for transfers between devices  158 us (21%)
  blocking collectives  66.4 us (9%)
  matrix products  61.6 us (8%)
  between operations  16.3 us (2%)
  starting transfers between devices  11.1 us (1%)
  loops' own time  10.7 us (1%)
    psum x1, waiting for transfers between devices, body(): summed = lax.psum((grad_terms[0], grad_terms[1], grad_terms[2]), 'ctx')  92.1 us
    reshape x8, local copies, waits for them, and re-layouts, toeplitz_tiles(): return repeated.reshape(groups, rows_count, period - 1)[:, :, :cols_count]  76.7 us
    ppermute x4, waiting for transfers between devices, passed_along(): return lax.ppermute(block, axis, route)  65.7 us
    reshape x8, local copies, waits for them, and re-layouts, lag_totals(): flattened.reshape(groups, rows_count, cols_count + 1)  63.8 us
    reduce_sum x3, other arithmetic, body(): short_parts.append(jnp.sum(grad_feat * earlier, axis=0))  43.2 us
    psum x1, blocking collectives, body(): summed = lax.psum((grad_terms[0], grad_terms[1], grad_terms[2]), 'ctx')  43.2 us
    while x32, local copies, waits for them, and re-layouts  38.8 us
    reduce_sum x8, other arithmetic, lag_totals(): jnp.sum(flattened.reshape(groups, rows_count, cols_count + 1), axis=1)  26.4 us
  transfers between devices with their start and end apart: 7, of which 3 were waited for; matrix products, arithmetic and copies ran while one was open for 18% of the time, Pallas kernels for 0%

commit v1 on v0

v1 whole, which is shorter than its diff:
```python
import functools

import jax
import jax.numpy as jnp
from jax import lax
from jax.experimental import pallas as pl
from jax.experimental.pallas import tpu as pltpu
from jax.sharding import PartitionSpec as P

GROUP = 16
LEN = 128
SHORT = 7
LANES = 128
FAR = 1 << 29
MESH = pl.DeviceIdType.MESH


def passed_along(block, axis, distance):
    devices = range(lax.axis_size(axis))
    route = [(i - distance, i) for i in devices if i - distance in devices]
    return lax.ppermute(block, axis, route)


def links(last):
    rows = lax.broadcasted_iota(jnp.int32, (last.shape[0], 1), 0)
    return [last <= rows - offset for offset in range(SHORT)]


def shifted_rows(tail, cur):
    whole = jnp.concatenate([tail[8:16].astype(jnp.float32), cur.astype(jnp.float32)], axis=0)
    return [
        (pltpu.roll(whole, offset, 0) if offset else whole)[8:] for offset in range(SHORT)
    ]


def featurize_kernel(last, q, k, v, qt, kt, vt, qw, kw, vw, up, qf, kf, vf, gate, glin):
    linked = links(last[...])

    def feature(cur, tail, taps):
        total = None
        for offset, rows in enumerate(shifted_rows(tail[...], cur[...])):
            term = taps[offset : offset + 1, :] * jnp.where(linked[offset], rows, 0.0)
            total = term if total is None else total + term
        return total

    query = feature(q, qt, qw)
    qf[...] = query
    key = feature(k, kt, kw)
    kf[...] = key
    value = feature(v, vt, vw)
    vf[...] = value
    gate[...] = (key * value).astype(jnp.bfloat16)
    glin[...] = (up[...].astype(jnp.float32) * query).astype(jnp.bfloat16)


def featurize(last, source, tail, taps, upstream):
    tok, channels = upstream.shape
    width = min(512, channels)
    steps = channels // width

    def part(rows, p):
        return pl.BlockSpec((rows, width), lambda i: (0, i + p * steps))

    own = pl.BlockSpec((tok, width), lambda i: (0, i))
    f32 = jax.ShapeDtypeStruct((tok, channels), jnp.float32)
    half = jax.ShapeDtypeStruct((tok, channels), jnp.bfloat16)
    return pl.pallas_call(
        featurize_kernel,
        grid=(steps,),
        in_specs=[pl.BlockSpec((tok, 1), lambda i: (0, 0))]
        + [part(tok, p) for p in range(3)]
        + [part(16, p) for p in range(3)]
        + [part(SHORT, p) for p in range(3)]
        + [own],
        out_specs=[own] * 5,
        out_shape=[f32, f32, f32, half, half],
        compiler_params=pltpu.CompilerParams(vmem_limit_bytes=40 << 20),
        name="featurize",
    )(last, source, source, source, tail, tail, tail, taps, taps, taps, upstream)


def conv_kernel(
    steps, last, last_row, skip, ahead, behind, gate, gate_prev, glin, glin_next,
    qf, kf, vf, up, q, k, v, qt, kt, vt, qw, kw, vw,
    mixed, grads, low, edge, short, skip_out, lag,
):
    step = pl.program_id(0)
    tok = gate.shape[0]
    win = 2 * tok
    linked = links(last[...])
    cols = lax.broadcasted_iota(jnp.int32, (tok, win), 1)
    rows = lax.broadcasted_iota(jnp.int32, (tok, win), 0)
    ahead_ok = last[...] <= cols - tok
    behind_ok = last_row[...] <= rows
    flip_r = lax.broadcasted_iota(jnp.int32, (tok, tok), 0)
    flip_c = lax.broadcasted_iota(jnp.int32, (tok, tok), 1)
    flip = (flip_r + flip_c == tok - 1).astype(jnp.bfloat16)
    own_gate, own_glin = gate[...], glin[...]
    gate_win = jnp.concatenate([gate_prev[...], own_gate], axis=0)
    glin_win = jnp.concatenate([own_glin, glin_next[...]], axis=0)
    glin_flip = jnp.dot(flip, own_glin, preferred_element_type=jnp.float32)
    flipped = ahead_flipped(last_row, tok)
    lane = lax.broadcasted_iota(jnp.int32, (tok, LANES), 1) // GROUP
    long_out = jnp.zeros((tok, LANES), jnp.float32)
    spread = jnp.zeros((tok, LANES), jnp.float32)
    for g in range(LANES // GROUP):
        mine = lane == g
        tile = jnp.broadcast_to(ahead[g : g + 1, :], (tok, win))
        tile = pltpu.roll(tile, 1, 1, stride=1, stride_axis=0)
        tile = jnp.where(ahead_ok, tile, 0.0).astype(jnp.bfloat16)
        out = jnp.dot(tile, gate_win, preferred_element_type=jnp.float32)
        long_out = jnp.where(mine, out, long_out)
        tile = jnp.broadcast_to(behind[g : g + 1, :], (tok, win))
        tile = pltpu.roll(tile, 0, 1, stride=1, stride_axis=0)
        tile = jnp.where(behind_ok, tile, 0.0).astype(jnp.bfloat16)
        out = jnp.dot(tile, glin_win, preferred_element_type=jnp.float32)
        spread = jnp.where(mine, out, spread)
        picked = jnp.where(mine, glin_flip, 0.0).astype(jnp.bfloat16)
        product = lax.dot_general(
            picked, gate_win, (((1,), (1,)), ((), ())), preferred_element_type=jnp.float32
        )
        product = jnp.where(flipped, product, 0.0)
        product = pltpu.roll(product, tok, 1, stride=1, stride_axis=0)
        lag[g : g + 1, :] = jnp.sum(product, axis=0, keepdims=True)[:, :LEN]
    gate_f = own_gate.astype(jnp.float32)
    query, key, value = qf[...], kf[...], vf[...]
    upstream = up[...].astype(jnp.float32)
    factor = skip[...]
    combined = long_out + factor * gate_f
    mixed[...] = (query * combined).astype(jnp.bfloat16)
    through = upstream * query
    skip_out[...] = jnp.sum(through * gate_f, axis=0, keepdims=True)
    grad_gate = spread + factor * through
    feats = (upstream * combined, grad_gate * value, grad_gate * key)
    for part, (grad, cur, tail, taps) in enumerate(
        zip(feats, (q, k, v), (qt, kt, vt), (qw, kw, vw))
    ):
        total = None
        at = pl.ds(pl.multiple_of((part * steps + step) * LANES, LANES), LANES)
        for offset, earlier in enumerate(shifted_rows(tail[...], cur[...])):
            kept = jnp.where(linked[offset], grad, 0.0)
            short[offset : offset + 1, at] = jnp.sum(kept * earlier, axis=0, keepdims=True)
            moved = jnp.concatenate(
                [jnp.zeros((8, LANES), jnp.float32), taps[offset : offset + 1, :] * kept], axis=0
            )
            if offset:
                moved = pltpu.roll(moved, tok + 8 - offset, 0)
            total = moved if total is None else total + moved
        grads[:, at] = total[8:].astype(jnp.bfloat16)
        low[:, at] = total[tok:]
        edge[:, at] = total[:8]


def ahead_flipped(last_row, tok):
    r = lax.broadcasted_iota(jnp.int32, (tok, tok), 0)
    c = lax.broadcasted_iota(jnp.int32, (tok, tok), 1)
    own = jnp.broadcast_to(last_row[:, :tok], (tok, tok))
    turned = jnp.sum(
        jnp.where(r + c == tok - 1, own, 0).astype(jnp.float32), axis=1, keepdims=True
    )
    cols = lax.broadcasted_iota(jnp.int32, (tok, 2 * tok), 1).astype(jnp.float32)
    return turned <= cols - tok


def convolve(last, last_row, skip, ahead, behind, gate, gate_prev, glin, glin_next,
             feats, upstream, source, tail, taps):
    tok, channels = upstream.shape
    steps = channels // LANES
    groups = LANES // GROUP

    def part(rows, p):
        return pl.BlockSpec((rows, LANES), lambda i: (0, i + p * steps))

    def fixed(shape):
        return pl.BlockSpec(shape, lambda i: (0, 0))

    own = part(tok, 0)
    f32 = jnp.float32
    return pl.pallas_call(
        functools.partial(conv_kernel, steps),
        grid=(steps,),
        in_specs=[fixed((tok, 1)), fixed((1, 2 * tok)), part(1, 0)]
        + [pl.BlockSpec((groups, 2 * tok), lambda i: (i, 0))] * 2
        + [own] * 8
        + [part(tok, p) for p in range(3)]
        + [part(16, p) for p in range(3)]
        + [part(SHORT, p) for p in range(3)],
        out_specs=[
            own,
            fixed((tok, 3 * channels)),
            fixed((8, 3 * channels)),
            fixed((8, 3 * channels)),
            fixed((SHORT, 3 * channels)),
            part(1, 0),
            pl.BlockSpec((groups, LEN), lambda i: (i, 0)),
        ],
        out_shape=[
            jax.ShapeDtypeStruct((tok, channels), jnp.bfloat16),
            jax.ShapeDtypeStruct((tok, 3 * channels), jnp.bfloat16),
            jax.ShapeDtypeStruct((8, 3 * channels), f32),
            jax.ShapeDtypeStruct((8, 3 * channels), f32),
            jax.ShapeDtypeStruct((SHORT, 3 * channels), f32),
            jax.ShapeDtypeStruct((1, channels), f32),
            jax.ShapeDtypeStruct((channels // GROUP, LEN), f32),
        ],
        compiler_params=pltpu.CompilerParams(vmem_limit_bytes=48 << 20),
        name="convolve",
    )(last, last_row, skip, ahead, behind, gate, gate_prev, glin, glin_next, *feats, upstream,
      source, source, source, tail, tail, tail, taps, taps, taps)


def reduce_kernel(
    m, n, scaling, x, out, pair, mine, parts, result, send0, recv0, send1, recv1, send2, recv2
):
    me, half = lax.axis_index("ctx"), lax.axis_index("fsdp")
    barrier = pltpu.get_barrier_semaphore()

    def greet_share(i, carry):
        pl.semaphore_signal(
            barrier, inc=1, device_id=(me, lax.rem(half + i, m)), device_id_type=MESH
        )
        return carry

    def greet(i, carry):
        pl.semaphore_signal(
            barrier, inc=1, device_id=(lax.rem(me + i, n), half), device_id_type=MESH
        )
        return carry

    lax.fori_loop(1, m, greet_share, 0)
    lax.fori_loop(1, n, greet, 0)
    pl.semaphore_wait(barrier, m + n - 2)

    def started(make, stop):
        def run(i, carry):
            make(i).start()
            return carry
        lax.fori_loop(1, stop, run, 0)

    def waited(make, stop):
        def run(i, carry):
            make(i).wait()
            return carry
        lax.fori_loop(1, stop, run, 0)

    def share(i):
        to = lax.rem(half + i, m)
        return pltpu.make_async_remote_copy(
            src_ref=x.at[to], dst_ref=pair.at[i], send_sem=send0.at[i], recv_sem=recv0.at[i],
            device_id=(me, to), device_id_type=MESH,
        )

    started(share, m)
    waited(share, m)
    owned = lax.fori_loop(1, m, lambda i, total: total + pair[i], x[half])
    mine[...] = (owned * scaling).astype(jnp.bfloat16)

    def scatter(i):
        to = lax.rem(me + i, n)
        return pltpu.make_async_remote_copy(
            src_ref=mine.at[to], dst_ref=parts.at[i], send_sem=send1.at[i], recv_sem=recv1.at[i],
            device_id=(to, half), device_id_type=MESH,
        )

    def gather(i):
        return pltpu.make_async_remote_copy(
            src_ref=result.at[me], dst_ref=result.at[me], send_sem=send2.at[i],
            recv_sem=recv2.at[i], device_id=(lax.rem(me + i, n), half), device_id_type=MESH,
        )

    started(scatter, n)
    waited(scatter, n)

    def add(i, total):
        return total + parts[i].astype(jnp.float32)

    total = lax.fori_loop(1, n, add, mine[me].astype(jnp.float32))
    result[me] = total.astype(jnp.bfloat16)
    started(gather, n)
    waited(gather, n)
    out[...] = result[...].astype(jnp.float32)


def reduced(packed, scaling):
    m, n, rows, _ = packed.shape
    half = pltpu.VMEM((n, rows, LANES), jnp.bfloat16)
    return pl.pallas_call(
        functools.partial(reduce_kernel, m, n, scaling),
        in_specs=[pl.BlockSpec(memory_space=pltpu.VMEM)],
        out_specs=pl.BlockSpec(memory_space=pltpu.VMEM),
        out_shape=jax.ShapeDtypeStruct((n, rows, LANES), jnp.float32),
        scratch_shapes=[
            pltpu.VMEM((m, n, rows, LANES), jnp.float32),
            half,
            half,
            half,
            pltpu.SemaphoreType.DMA((m,)),
            pltpu.SemaphoreType.DMA((m,)),
            pltpu.SemaphoreType.DMA((n,)),
            pltpu.SemaphoreType.DMA((n,)),
            pltpu.SemaphoreType.DMA((n,)),
            pltpu.SemaphoreType.DMA((n,)),
        ],
        compiler_params=pltpu.CompilerParams(
            collective_id=0, has_side_effects=True, vmem_limit_bytes=32 << 20
        ),
        name="reduce",
    )(packed)


def body(proj, short_taps, long_filter, skip, grad_out, starts):
    source, upstream = proj[0], grad_out[0]
    tok, channels = upstream.shape
    count, me = lax.axis_size("ctx"), lax.axis_index("ctx")
    pairs = lax.axis_size("fsdp")
    taps = lax.all_gather(short_taps, "fsdp", axis=1, tiled=True)
    filt = lax.all_gather(long_filter, "fsdp", axis=1, tiled=True)
    factor = lax.all_gather(skip, "fsdp", axis=0, tiled=True)
    lists = lax.all_gather(starts[0, 0], "ctx")
    tail = passed_along(source[tok - 16 :], "ctx", 1)
    places = jnp.arange(count, dtype=jnp.int32)
    positions = jnp.arange(tok, dtype=jnp.int32)
    absolute = jnp.where(lists < tok, lists + (places * tok)[:, None], -FAR)

    def last_of(device):
        first = device * tok
        seen = jnp.where(
            (absolute.reshape(-1)[None, :] <= first + positions[:, None]),
            absolute.reshape(-1)[None, :], -FAR,
        )
        return jnp.max(seen, axis=1) - first

    last = last_of(me)
    later = jnp.where(me < count - 1, last_of(me + 1) + tok, FAR)
    last_row = jnp.concatenate([last, later])[None, :]
    last = last[:, None]
    rows = filt.T
    empty = jnp.zeros_like(rows)
    ahead = jnp.concatenate([rows[:, ::-1], empty], axis=1)
    behind = jnp.concatenate([rows, empty], axis=1)

    qf, kf, vf, gate, glin = featurize(last, source, tail, taps, upstream)
    gate_prev = passed_along(gate, "ctx", 1)
    glin_next = passed_along(glin, "ctx", -1)
    mixed, grads, low, edge, short, skip_part, lag = convolve(
        last, last_row, factor[None], ahead, behind, gate, gate_prev, glin, glin_next,
        (qf, kf, vf), upstream, source, tail, taps,
    )
    returned = passed_along(edge[8 - (SHORT - 1) :].astype(jnp.bfloat16), "ctx", -1)
    fixed = low[8 - (SHORT - 1) :] + returned.astype(jnp.float32)
    grads = lax.dynamic_update_slice(grads, fixed.astype(jnp.bfloat16), (tok - (SHORT - 1), 0))

    scaling = float(pairs * count * tok) ** (-0.5)
    own = 3 * channels // pairs
    groups = channels // GROUP
    long_grad = lag[:, ::-1].T
    sizes = (SHORT * own, LEN * (groups // pairs), channels // pairs)
    flat = jnp.concatenate(
        [
            short.reshape(SHORT, pairs, own).transpose(1, 0, 2).reshape(pairs, -1),
            long_grad.reshape(LEN, pairs, groups // pairs).transpose(1, 0, 2).reshape(pairs, -1),
            skip_part.reshape(pairs, -1),
        ],
        axis=1,
    )
    unit = count * 16 * LANES
    padded = -(-flat.shape[1] // unit) * unit
    flat = jnp.pad(flat, ((0, 0), (0, padded - flat.shape[1])))
    summed = reduced(flat.reshape(pairs, count, -1, LANES), scaling).reshape(-1)
    a, b, c = sizes
    return (
        mixed[None],
        grads[None],
        summed[:a].reshape(SHORT, own),
        summed[a : a + b].reshape(LEN, groups // pairs),
        summed[a + b : a + b + c],
    )


def solution(mesh):
    window = P("fsdp", "ctx", None)
    return jax.shard_map(
        body,
        mesh=mesh,
        in_specs=(window, P(None, "fsdp"), P(None, "fsdp"), P("fsdp"), window, window),
        out_specs=(window, window, P(None, "fsdp"), P(None, "fsdp"), P("fsdp")),
        check_vma=False,
    )
```

time: 768 us -> 203 us (0.26)
  local copies, waits for them, and re-layouts: 280 us -> 17.8 us
  other arithmetic: 161 us -> 1.1 us
  waiting for transfers between devices: 158 us -> 39.3 us
  Pallas kernels: 0 us -> 85.5 us
  matrix products: 61.6 us -> 0 us
  blocking collectives: 66.4 us -> 48.3 us
  between operations: 16.3 us -> 0.86 us
  loops' own time: 10.7 us -> 0 us
    reshape x16 -> x3, local copies, waits for them, and re-layouts: 141 us -> 2.05 us  [the longest x1 1.32 us: body(): short.reshape(SHORT, pairs, own).transpose(1, 0, 2).reshape(pairs, -1)]
    psum x1 -> x0, waiting for transfers between devices: 92.1 us -> none  [body(): summed = lax.psum((grad_terms[0], grad_terms[1], grad_terms[2]), 'ctx')]
    pallas_call x0 -> x3, Pallas kernels: none -> 85.5 us  [the longest x1 56.9 us: convolve(): pl.pallas_call(functools.partial(conv_kernel, steps), grid=(steps,), in_s...]
    reduce_sum x12 -> x0, other arithmetic: 71.7 us -> none  [the longest x3 43.2 us: body(): short_parts.append(jnp.sum(grad_feat * earlier, axis=0))]
    dot_general x24 -> x0, matrix products: 61.6 us -> none  [the longest x8 24.4 us: joint_block(): jnp.einsum('gcs,gts->gct', win_blk, tiles, preferred_element_type=jnp.flo...]
    add x2, other arithmetic: 51.4 us -> 0.01 us  [last_of(): first + positions[:, None]]
    psum x1 -> x0, blocking collectives: 43.2 us -> none  [body(): summed = lax.psum((grad_terms[0], grad_terms[1], grad_terms[2]), 'ctx')]
    all_gather x3 -> x4, blocking collectives: 5.75 us -> 48.3 us  [the longest x1 42.3 us: body(): lists = lax.all_gather(starts[0, 0], 'ctx')]
  transfers between devices with their start and end apart: 7 -> 4, of which waited for: 3 -> 2; matrix products, arithmetic and copies ran while one was open for 18% -> 1% of each run, Pallas kernels for 0% -> 9%
where the time goes in v1:
time: 203 us
  Pallas kernels  85.5 us (42%)
  blocking collectives  48.3 us (24%)
  waiting for transfers between devices  39.3 us (19%)
  local copies, waits for them, and re-layouts  17.8 us (9%)
  starting transfers between devices  9.72 us (5%)
    pallas_call x1, Pallas kernels, convolve(): pl.pallas_call(functools.partial(conv_kernel, steps), grid=(steps,), in_s...  56.9 us
    all_gather x1, blocking collectives, body(): lists = lax.all_gather(starts[0, 0], 'ctx')  42.3 us
    ppermute x4, waiting for transfers between devices, passed_along(): return lax.ppermute(block, axis, route)  39.3 us
    pallas_call x1, Pallas kernels, reduced(): pl.pallas_call(functools.partial(reduce_kernel, m, n, scaling), in_specs=...  18 us
    pallas_call x1, Pallas kernels, featurize(): pl.pallas_call(featurize_kernel, grid=(steps,), in_specs=[pl.BlockSpec((t...  10.6 us
    ppermute x4, starting transfers between devices, passed_along(): return lax.ppermute(block, axis, route)  9.72 us
    unnamed x21, local copies, waits for them, and re-layouts  8.8 us
  transfers between devices with their start and end apart: 4, of which 2 were waited for; matrix products, arithmetic and copies ran while one was open for 1% of the time, Pallas kernels for 9%

profile of v1, /device:TPU:0, one launch (start us, length us, event | category | flops | bytes accessed | tf_op | source)
XLA Modules:
  0.0 202.6 jit_solution(2455299707800344055)
XLA Ops:
  0.6 1.0 slice_bitcast_fusion
  1.7 4.9 %collective-permute-start = (bf16[16,12288]{1,0:T(8,128)(2,1)S(1)}, bf16[16,12288]{1,0:T(8,128)(2,1)S(1)}, u32[]{:S(2)}, u32[]{:S(2)}) collective-permute-start(bf16[16,12288]{1,0:T(8,128)(2,1)S(1)} %slice_bitcast_fusion), channel_id=1, source_target_pairs={{0,2},{2,4},{4,6},{6,8},{8,10},{10,12},{12,14},{14,16},{16,18},{18... | collective-permute-start | bytes 1179656 | tf_op jit(solution)/shard_map/ppermute | solution.py:21
  6.6 42.3 %all-gather = s32[16,1,4]{2,1,0:T(1,128)S(1)} all-gather(s32[1,1,4]{2,1,0:T(1,128)} %param.11), channel_id=2, replica_groups=mesh['ctx'=16,'fsdp'=2] {'ctx'}, dimensions={0}, use_global_device_ids=true | all-gather | bytes 272 | tf_op jit(solution)/shard_map/all_gather | solution.py:319
  49.4 2.3 %all_gather.15.qw.kw.vw = f32[7,12288]{1,0:T(8,128)S(1)} all-gather(f32[7,6144]{1,0:T(8,128)} %param.7), channel_id=1, replica_groups=mesh['ctx'=16,'fsdp'=2] {'fsdp'}, dimensions={1}, use_global_device_ids=true | all-gather | bytes 516096 | tf_op jit(solution)/shard_map/all_gather | solution.py:316
  51.7 1.9 copy-done
  53.6 1.2 copy-done.1
  54.8 10.6 %featurize.1 = (f32[128,4096]{1,0:T(8,128)S(1)}, f32[128,4096]{1,0:T(8,128)S(1)}, f32[128,4096]{1,0:T(8,128)S(1)}, bf16[128,4096]{1,0:T(8,128)(2,1)S(1)}, bf16[128,4096]{1,0:T(8,128)(2,1)S(1)}) custom-call(s32[128,1]{1,0:T(8,128)S(1)} %copy.33.last, bf16[128,12288]{1,0:T(8,128)(2,1)S(1)} %bitcast.40, bf16[128,12288]{1,0:T(8,128)(2,1)S(1)} %bitcast.41, ...), custom_call_target="tpu_custom_call" | custom-call | tf_op jit(solution)/shard_map/featurize/pallas_call | solution.py:67
  65.4 1.3 copy-done.2
  66.7 1.3 copy-done.3
  68.0 1.3 copy-done.4
  69.3 2.3 %collective-permute-start.1 = (bf16[128,4096]{1,0:T(8,128)(2,1)S(1)}, bf16[128,4096]{1,0:T(8,128)(2,1)}, u32[]{:S(2)}, u32[]{:S(2)}) collective-permute-start(bf16[128,4096]{1,0:T(8,128)(2,1)S(1)} %get-tuple-element.17.gate), channel_id=1, source_target_pairs={{0,2},{2,4},{4,6},{6,8},{8,10},{10,12},{12,14},{14,16},{16,18},{18... | collective-permute-start | bytes 3145736 | tf_op jit(solution)/shard_map/ppermute | solution.py:21
  71.6 1.3 collective-permute-start.2
  73.0 1.9 all_gather.14
  75.2 1.8 all_gather.13
  77.0 39.1 %collective-permute-done.1.gate_prev = bf16[128,4096]{1,0:T(8,128)(2,1)} collective-permute-done((bf16[128,4096]{1,0:T(8,128)(2,1)S(1)}, bf16[128,4096]{1,0:T(8,128)(2,1)}, u32[]{:S(2)}, u32[]{:S(2)}) %collective-permute-start.1) | collective-permute-done | bytes 1048608 | tf_op jit(solution)/shard_map/ppermute | solution.py:21
  116.3 56.9 %convolve.1 = (bf16[128,4096]{1,0:T(8,128)(2,1)}, bf16[128,12288]{1,0:T(8,128)(2,1)}, f32[8,12288]{1,0:T(8,128)S(1)}, f32[8,12288]{1,0:T(8,128)S(1)}, f32[7,1228...) custom-call(s32[128,1]{1,0:T(8,128)S(1)} %copy.33.last, s32[1,256]{1,0:T(1,128)S(1)} %bitcast.50, ...), custom_call_target="tpu_custom_call" | custom-call | tf_op jit(solution)/shard_map/convolve/pallas_call | solution.py:179
  173.2 0.7 copy-done.5
  174.0 0.7 copy-done.6
  175.1 1.3 reshape.64
  177.7 1.0 slice.42
  178.7 1.3 collective-permute-start.3
  180.3 18.0 %reduce.5 = f32[16,32,128]{2,1,0:T(8,128)S(1)} custom-call(f32[2,16,32,128]{3,2,1,0:T(8,128)S(1)} %bitcast.45), custom_call_target="tpu_custom_call" | custom-call | tf_op jit(solution)/shard_map/reduce/pallas_call | solution.py:287
  198.9 0.7 reshape.71
  200.3 2.3 %dynamic_update_slice.4 = bf16[1,128,12288]{2,1,0:T(8,128)(2,1)} dynamic-update-slice(bf16[1,128,12288]{2,1,0:T(8,128)(2,1)} %bitcast.58, bf16[1,6,12288]{2,1,0:T(8,128)(2,1)S(1)} %fusion.1, s32[]{:T(128)} %constant.10.clone.1, s32[]{:T(128)} %constant.28.clone.1, s32[]{:T(128)} %constant.10.clone.1) | dynamic-update-slice | bytes 294916 | tf_op jit(solution)/shard_map/dynamic_update_slice | solution.py:351
  (41 shorter events, 4.2 us)
Async XLA Ops:
  1.7 50.0 %collective-permute-start = (bf16[16,12288]{1,0:T(8,128)(2,1)S(1)}, bf16[16,12288]{1,0:T(8,128)(2,1)S(1)}, u32[]{:S(2)}, u32[]{:S(2)}) collective-permute-start(bf16[16,12288]{1,0:T(8,128)(2,1)S(1)} %slice_bitcast_fusion), channel_id=1, source_target_pairs={{0,2},{2,4},{4,6},{6,8},{8,10},{10,12},{12,14},{14,16},{16,18},{18... | collective-permute-start | bytes 1179656 | tf_op jit(solution)/shard_map/ppermute | solution.py:21
  51.7 1.9 copy-start
  53.6 1.2 copy-start.1
  54.8 18.1 %copy-start.7 = (f32[128,128]{1,0:T(8,128)S(1)}, f32[128,128]{1,0:T(8,128)}, u32[]{:S(2)}) copy-start(f32[128,128]{1,0:T(8,128)} %param.8) | copy-start | bytes 196612
  54.8 20.4 %copy-start.8 = (f32[2048]{0:T(1024)S(1)}, f32[2048]{0:T(1024)}, u32[]{:S(2)}) copy-start(f32[2048]{0:T(1024)} %param.9) | copy-start | bytes 24580
  65.4 1.3 copy-start.2
  66.7 1.3 copy-start.3
  68.0 1.3 copy-start.4
  69.3 46.7 %collective-permute-start.1 = (bf16[128,4096]{1,0:T(8,128)(2,1)S(1)}, bf16[128,4096]{1,0:T(8,128)(2,1)}, u32[]{:S(2)}, u32[]{:S(2)}) collective-permute-start(bf16[128,4096]{1,0:T(8,128)(2,1)S(1)} %get-tuple-element.17.gate), channel_id=1, source_target_pairs={{0,2},{2,4},{4,6},{6,8},{8,10},{10,12},{12,14},{14,16},{16,18},{18... | collective-permute-start | bytes 3145736 | tf_op jit(solution)/shard_map/ppermute | solution.py:21
  71.6 44.7 %collective-permute-start.2 = (bf16[128,4096]{1,0:T(8,128)(2,1)S(1)}, bf16[128,4096]{1,0:T(8,128)(2,1)}, u32[]{:S(2)}, u32[]{:S(2)}) collective-permute-start(bf16[128,4096]{1,0:T(8,128)(2,1)S(1)} %get-tuple-element.18.glin), channel_id=1, source_target_pairs={{2,0},{4,2},{6,4},{8,6},{10,8},{12,10},{14,12},{16,14},{18,16},{20... | collective-permute-start | bytes 3145736 | tf_op jit(solution)/shard_map/ppermute | solution.py:21
  173.2 0.8 copy-start.5
  174.0 0.7 copy-start.6
  178.7 21.5 %collective-permute-start.3 = (bf16[6,12288]{1,0:T(8,128)(2,1)S(1)}, bf16[6,12288]{1,0:T(8,128)(2,1)S(1)}, u32[]{:S(2)}, u32[]{:S(2)}) collective-permute-start(bf16[6,12288]{1,0:T(8,128)(2,1)S(1)} %slice.42), channel_id=1, source_target_pairs={{2,0},{4,2},{6,4},{8,6},{10,8},{12,10},{14,12},{16,14},{18,16},{20... | collective-permute-start | bytes 442376 | tf_op jit(solution)/shard_map/ppermute | solution.py:21

commit v2 on v1

--- a/solution.py
+++ b/solution.py
@@ -12,6 +12,7 @@
 SHORT = 7
 LANES = 128
 FAR = 1 << 29
+CHUNKS = 4
 MESH = pl.DeviceIdType.MESH
 
 
@@ -31,6 +32,12 @@
     return [
         (pltpu.roll(whole, offset, 0) if offset else whole)[8:] for offset in range(SHORT)
     ]
+
+
+def exchange_matrix(size):
+    r = lax.broadcasted_iota(jnp.int32, (size, size), 0)
+    c = lax.broadcasted_iota(jnp.int32, (size, size), 1)
+    return (r + c == size - 1).astype(jnp.bfloat16)
 
 
 def featurize_kernel(last, q, k, v, qt, kt, vt, qw, kw, vw, up, qf, kf, vf, gate, glin):
@@ -50,16 +57,20 @@
     value = feature(v, vt, vw)
     vf[...] = value
     gate[...] = (key * value).astype(jnp.bfloat16)
-    glin[...] = (up[...].astype(jnp.float32) * query).astype(jnp.bfloat16)
-
-
-def featurize(last, source, tail, taps, upstream):
+    through = (up[...].astype(jnp.float32) * query).astype(jnp.bfloat16)
+    turned = jnp.dot(exchange_matrix(through.shape[0]), through, preferred_element_type=jnp.float32)
+    glin[...] = turned.astype(jnp.bfloat16)
+
+
+def featurize(chunk, chunks, last, source, tail, taps, upstream):
     tok, channels = upstream.shape
-    width = min(512, channels)
-    steps = channels // width
+    width = min(512, channels // chunks)
+    whole = channels // width
+    steps = whole // chunks
+    channels = channels // chunks
 
     def part(rows, p):
-        return pl.BlockSpec((rows, width), lambda i: (0, i + p * steps))
+        return pl.BlockSpec((rows, width), lambda i: (0, i + chunk * steps + p * whole))
 
     own = pl.BlockSpec((tok, width), lambda i: (0, i))
     f32 = jax.ShapeDtypeStruct((tok, channels), jnp.float32)
@@ -71,7 +82,7 @@
         + [part(tok, p) for p in range(3)]
         + [part(16, p) for p in range(3)]
         + [part(SHORT, p) for p in range(3)]
-        + [own],
+        + [part(tok, 0)],
         out_specs=[own] * 5,
         out_shape=[f32, f32, f32, half, half],
         compiler_params=pltpu.CompilerParams(vmem_limit_bytes=40 << 20),
@@ -80,48 +91,57 @@
 
 
 def conv_kernel(
-    steps, last, last_row, skip, ahead, behind, gate, gate_prev, glin, glin_next,
+    last, last_turned, row_turned, skip, ahead, gate, gate_prev, glin, glin_next,
     qf, kf, vf, up, q, k, v, qt, kt, vt, qw, kw, vw,
-    mixed, grads, low, edge, short, skip_out, lag,
+    mixed, gq, gk, gv, low, edge, short, skip_out, lag, tiles_f, tiles_b, picked,
 ):
-    step = pl.program_id(0)
     tok = gate.shape[0]
-    win = 2 * tok
+    count = LANES // GROUP
     linked = links(last[...])
-    cols = lax.broadcasted_iota(jnp.int32, (tok, win), 1)
-    rows = lax.broadcasted_iota(jnp.int32, (tok, win), 0)
-    ahead_ok = last[...] <= cols - tok
-    behind_ok = last_row[...] <= rows
-    flip_r = lax.broadcasted_iota(jnp.int32, (tok, tok), 0)
-    flip_c = lax.broadcasted_iota(jnp.int32, (tok, tok), 1)
-    flip = (flip_r + flip_c == tok - 1).astype(jnp.bfloat16)
+    cols = lax.broadcasted_iota(jnp.int32, (tok, tok), 1)
+    rows = lax.broadcasted_iota(jnp.int32, (tok, tok), 0)
+    below = cols <= rows
+    fwd_prev = jnp.logical_and(jnp.logical_not(below), last[...] <= cols - tok)
+    fwd_own = jnp.logical_and(below, last[...] <= cols)
+    turned = tok - 1 - rows
+    bwd_next = jnp.logical_and(jnp.logical_not(below), row_turned[:, :tok] <= turned)
+    bwd_own = jnp.logical_and(below, row_turned[:, tok:] <= turned)
+    lag_prev = jnp.logical_and(cols > turned, last_turned[...] <= cols - tok)
+    lag_own = jnp.logical_and(cols <= turned, last_turned[...] <= cols)
     own_gate, own_glin = gate[...], glin[...]
     gate_win = jnp.concatenate([gate_prev[...], own_gate], axis=0)
-    glin_win = jnp.concatenate([own_glin, glin_next[...]], axis=0)
-    glin_flip = jnp.dot(flip, own_glin, preferred_element_type=jnp.float32)
-    flipped = ahead_flipped(last_row, tok)
+    glin_win = jnp.concatenate([glin_next[...], own_glin], axis=0)
     lane = lax.broadcasted_iota(jnp.int32, (tok, LANES), 1) // GROUP
-    long_out = jnp.zeros((tok, LANES), jnp.float32)
-    spread = jnp.zeros((tok, LANES), jnp.float32)
-    for g in range(LANES // GROUP):
-        mine = lane == g
-        tile = jnp.broadcast_to(ahead[g : g + 1, :], (tok, win))
+    for g in range(count):
+        at = slice(g * tok, (g + 1) * tok)
+        tile = jnp.broadcast_to(ahead[g : g + 1, :], (tok, LEN))
         tile = pltpu.roll(tile, 1, 1, stride=1, stride_axis=0)
-        tile = jnp.where(ahead_ok, tile, 0.0).astype(jnp.bfloat16)
-        out = jnp.dot(tile, gate_win, preferred_element_type=jnp.float32)
-        long_out = jnp.where(mine, out, long_out)
-        tile = jnp.broadcast_to(behind[g : g + 1, :], (tok, win))
-        tile = pltpu.roll(tile, 0, 1, stride=1, stride_axis=0)
-        tile = jnp.where(behind_ok, tile, 0.0).astype(jnp.bfloat16)
-        out = jnp.dot(tile, glin_win, preferred_element_type=jnp.float32)
-        spread = jnp.where(mine, out, spread)
-        picked = jnp.where(mine, glin_flip, 0.0).astype(jnp.bfloat16)
-        product = lax.dot_general(
-            picked, gate_win, (((1,), (1,)), ((), ())), preferred_element_type=jnp.float32
-        )
-        product = jnp.where(flipped, product, 0.0)
-        product = pltpu.roll(product, tok, 1, stride=1, stride_axis=0)
-        lag[g : g + 1, :] = jnp.sum(product, axis=0, keepdims=True)[:, :LEN]
+        tiles_f[at, :tok] = jnp.where(fwd_prev, tile, 0.0).astype(jnp.bfloat16)
+        tiles_f[at, tok:] = jnp.where(fwd_own, tile, 0.0).astype(jnp.bfloat16)
+        tiles_b[at, :tok] = jnp.where(bwd_next, tile, 0.0).astype(jnp.bfloat16)
+        tiles_b[at, tok:] = jnp.where(bwd_own, tile, 0.0).astype(jnp.bfloat16)
+        picked[at, :] = jnp.where(lane == g, own_glin.astype(jnp.float32), 0.0).astype(jnp.bfloat16)
+    out_f = jnp.dot(tiles_f[...], gate_win, preferred_element_type=jnp.float32)
+    out_b = jnp.dot(tiles_b[...], glin_win, preferred_element_type=jnp.float32)
+    product = lax.dot_general(
+        picked[...], gate_win, (((1,), (1,)), ((), ())), preferred_element_type=jnp.float32
+    )
+    long_out, spread = out_f[:tok], out_b[:tok]
+    for g in range(count):
+        at = slice(g * tok, (g + 1) * tok)
+        if g:
+            long_out = jnp.where(lane == g, out_f[at], long_out)
+            spread = jnp.where(lane == g, out_b[at], spread)
+        folded = jnp.where(lag_prev, product[at, :tok], 0.0)
+        folded = jnp.where(lag_own, product[at, tok:], folded)
+        folded = pltpu.roll(folded, 0, 1, stride=1, stride_axis=0)
+        lag[g : g + 1, :] = jnp.sum(folded, axis=0, keepdims=True)
+    flip = exchange_matrix(tok)
+    high = spread.astype(jnp.bfloat16)
+    rest = (spread - high.astype(jnp.float32)).astype(jnp.bfloat16)
+    spread = jnp.dot(flip, high, preferred_element_type=jnp.float32) + jnp.dot(
+        flip, rest, preferred_element_type=jnp.float32
+    )
     gate_f = own_gate.astype(jnp.float32)
     query, key, value = qf[...], kf[...], vf[...]
     upstream = up[...].astype(jnp.float32)
@@ -132,81 +152,183 @@
     skip_out[...] = jnp.sum(through * gate_f, axis=0, keepdims=True)
     grad_gate = spread + factor * through
     feats = (upstream * combined, grad_gate * value, grad_gate * key)
-    for part, (grad, cur, tail, taps) in enumerate(
-        zip(feats, (q, k, v), (qt, kt, vt), (qw, kw, vw))
+    for part, (grad, cur, tail, taps, out) in enumerate(
+        zip(feats, (q, k, v), (qt, kt, vt), (qw, kw, vw), (gq, gk, gv))
     ):
         total = None
-        at = pl.ds(pl.multiple_of((part * steps + step) * LANES, LANES), LANES)
         for offset, earlier in enumerate(shifted_rows(tail[...], cur[...])):
             kept = jnp.where(linked[offset], grad, 0.0)
-            short[offset : offset + 1, at] = jnp.sum(kept * earlier, axis=0, keepdims=True)
+            short[part, offset : offset + 1, :] = jnp.sum(kept * earlier, axis=0, keepdims=True)
             moved = jnp.concatenate(
                 [jnp.zeros((8, LANES), jnp.float32), taps[offset : offset + 1, :] * kept], axis=0
             )
             if offset:
                 moved = pltpu.roll(moved, tok + 8 - offset, 0)
             total = moved if total is None else total + moved
-        grads[:, at] = total[8:].astype(jnp.bfloat16)
-        low[:, at] = total[tok:]
-        edge[:, at] = total[:8]
-
-
-def ahead_flipped(last_row, tok):
-    r = lax.broadcasted_iota(jnp.int32, (tok, tok), 0)
-    c = lax.broadcasted_iota(jnp.int32, (tok, tok), 1)
-    own = jnp.broadcast_to(last_row[:, :tok], (tok, tok))
-    turned = jnp.sum(
-        jnp.where(r + c == tok - 1, own, 0).astype(jnp.float32), axis=1, keepdims=True
-    )
-    cols = lax.broadcasted_iota(jnp.int32, (tok, 2 * tok), 1).astype(jnp.float32)
-    return turned <= cols - tok
-
-
-def convolve(last, last_row, skip, ahead, behind, gate, gate_prev, glin, glin_next,
-             feats, upstream, source, tail, taps):
+        out[...] = total[8:].astype(jnp.bfloat16)
+        low[part] = total[tok:]
+        edge[part] = total[:8]
+
+
+def convolve(chunk, chunks, last, last_turned, row_turned, skip, ahead, gate, gate_prev, glin,
+             glin_next, feats, upstream, source, tail, taps):
     tok, channels = upstream.shape
-    steps = channels // LANES
+    whole = channels // LANES
+    steps = whole // chunks
+    channels = channels // chunks
     groups = LANES // GROUP
 
     def part(rows, p):
-        return pl.BlockSpec((rows, LANES), lambda i: (0, i + p * steps))
+        return pl.BlockSpec((rows, LANES), lambda i: (0, i + chunk * steps + p * whole))
 
     def fixed(shape):
         return pl.BlockSpec(shape, lambda i: (0, 0))
 
-    own = part(tok, 0)
+    def three(rows):
+        return pl.BlockSpec((3, rows, LANES), lambda i: (0, 0, i))
+
+    own = pl.BlockSpec((tok, LANES), lambda i: (0, i))
     f32 = jnp.float32
+    half = jax.ShapeDtypeStruct((tok, channels), jnp.bfloat16)
+    rows = 2 * groups * tok * channels * 2 * tok
     return pl.pallas_call(
-        functools.partial(conv_kernel, steps),
+        conv_kernel,
         grid=(steps,),
-        in_specs=[fixed((tok, 1)), fixed((1, 2 * tok)), part(1, 0)]
-        + [pl.BlockSpec((groups, 2 * tok), lambda i: (i, 0))] * 2
-        + [own] * 8
+        in_specs=[fixed((tok, 1)), fixed((tok, 1)), fixed((1, 2 * tok)), part(1, 0)]
+        + [pl.BlockSpec((groups, LEN), lambda i: (i + chunk * steps, 0))]
+        + [own] * 7
+        + [part(tok, 0)]
         + [part(tok, p) for p in range(3)]
         + [part(16, p) for p in range(3)]
         + [part(SHORT, p) for p in range(3)],
-        out_specs=[
-            own,
-            fixed((tok, 3 * channels)),
-            fixed((8, 3 * channels)),
-            fixed((8, 3 * channels)),
-            fixed((SHORT, 3 * channels)),
-            part(1, 0),
-            pl.BlockSpec((groups, LEN), lambda i: (i, 0)),
-        ],
-        out_shape=[
-            jax.ShapeDtypeStruct((tok, channels), jnp.bfloat16),
-            jax.ShapeDtypeStruct((tok, 3 * channels), jnp.bfloat16),
-            jax.ShapeDtypeStruct((8, 3 * channels), f32),
-            jax.ShapeDtypeStruct((8, 3 * channels), f32),
-            jax.ShapeDtypeStruct((SHORT, 3 * channels), f32),
+        out_specs=[own] * 4
+        + [three(8), three(8), three(SHORT)]
+        + [pl.BlockSpec((1, LANES), lambda i: (0, i)), pl.BlockSpec((groups, LEN), lambda i: (i, 0))],
+        out_shape=[half] * 4 + [
+            jax.ShapeDtypeStruct((3, 8, channels), f32),
+            jax.ShapeDtypeStruct((3, 8, channels), f32),
+            jax.ShapeDtypeStruct((3, SHORT, channels), f32),
             jax.ShapeDtypeStruct((1, channels), f32),
             jax.ShapeDtypeStruct((channels // GROUP, LEN), f32),
         ],
-        compiler_params=pltpu.CompilerParams(vmem_limit_bytes=48 << 20),
+        scratch_shapes=[
+            pltpu.VMEM((groups * tok, 2 * tok), jnp.bfloat16),
+            pltpu.VMEM((groups * tok, 2 * tok), jnp.bfloat16),
+            pltpu.VMEM((groups * tok, LANES), jnp.bfloat16),
+        ],
+        compiler_params=pltpu.CompilerParams(vmem_limit_bytes=40 << 20),
+        cost_estimate=pl.CostEstimate(flops=3 * rows, bytes_accessed=22 * tok * channels, transcendentals=0),
         name="convolve",
-    )(last, last_row, skip, ahead, behind, gate, gate_prev, glin, glin_next, *feats, upstream,
-      source, source, source, tail, tail, tail, taps, taps, taps)
+    )(last, last_turned, row_turned, skip, ahead, gate, gate_prev, glin, glin_next, *feats,
+      upstream, source, source, source, tail, tail, tail, taps, taps, taps)
+
+
+def entry_kernel(m, n, proj, taps, filt, skip, starts, tail, taps_all, filt_all, skip_all, lists,
+                 tail_sems, start_send, start_recv, share_send, share_recv):
+    me, half = lax.axis_index("ctx"), lax.axis_index("fsdp")
+    tok, own, skips = proj.shape[0], taps.shape[1], skip.shape[1]
+    barrier = pltpu.get_barrier_semaphore()
+
+    def greet_share(i, carry):
+        pl.semaphore_signal(
+            barrier, inc=1, device_id=(me, lax.rem(half + i, m)), device_id_type=MESH
+        )
+        return carry
+
+    def greet(i, carry):
+        pl.semaphore_signal(
+            barrier, inc=1, device_id=(lax.rem(me + i, n), half), device_id_type=MESH
+        )
+        return carry
+
+    lax.fori_loop(1, m, greet_share, 0)
+    lax.fori_loop(1, n, greet, 0)
+    pl.semaphore_wait(barrier, m + n - 2)
+    taps_at = pl.ds(pl.multiple_of(half * own, LANES), own)
+    skip_at = pl.ds(pl.multiple_of(half * skips, LANES), skips)
+
+    def first(i):
+        return pltpu.make_async_remote_copy(
+            src_ref=starts, dst_ref=lists.at[me], send_sem=start_send.at[i],
+            recv_sem=start_recv.at[i], device_id=(lax.rem(me + i, n), half), device_id_type=MESH,
+        )
+
+    def shares(i):
+        to = lax.rem(half + i, m)
+        pairs = (
+            (taps, taps_all.at[:, taps_at]),
+            (filt, filt_all.at[half]),
+            (skip, skip_all.at[:, skip_at]),
+        )
+        return [
+            pltpu.make_async_remote_copy(
+                src_ref=src, dst_ref=dst, send_sem=share_send.at[j, i],
+                recv_sem=share_recv.at[j, i], device_id=(me, to), device_id_type=MESH,
+            )
+            for j, (src, dst) in enumerate(pairs)
+        ]
+
+    onward = pltpu.make_async_remote_copy(
+        src_ref=proj.at[tok - 16 : tok], dst_ref=tail, send_sem=tail_sems.at[0],
+        recv_sem=tail_sems.at[1], device_id=(lax.rem(me + 1, n), half), device_id_type=MESH,
+    )
+    onward.start()
+
+    def start_first(i, carry):
+        first(i).start()
+        return carry
+
+    def start_share(i, carry):
+        for copy in shares(i):
+            copy.start()
+        return carry
+
+    def wait_first(i, carry):
+        first(i).wait()
+        return carry
+
+    def wait_share(i, carry):
+        for copy in shares(i):
+            copy.wait()
+        return carry
+
+    lax.fori_loop(1, n, start_first, 0)
+    lax.fori_loop(1, m, start_share, 0)
+    lists[me] = starts[...]
+    taps_all[:, taps_at] = taps[...]
+    filt_all[half] = filt[...]
+    skip_all[:, skip_at] = skip[...]
+    lax.fori_loop(1, n, wait_first, 0)
+    lax.fori_loop(1, m, wait_share, 0)
+    onward.wait()
+
+
+def entry(m, n, source, taps, filt, skip, starts):
+    vmem = pl.BlockSpec(memory_space=pltpu.VMEM)
+    f32 = jnp.float32
+    return pl.pallas_call(
+        functools.partial(entry_kernel, m, n),
+        in_specs=[pl.BlockSpec(memory_space=pl.ANY)] + [vmem] * 4,
+        out_specs=[vmem] * 5,
+        out_shape=[
+            jax.ShapeDtypeStruct((16, source.shape[1]), source.dtype),
+            jax.ShapeDtypeStruct((SHORT, m * taps.shape[1]), f32),
+            jax.ShapeDtypeStruct((m,) + filt.shape, f32),
+            jax.ShapeDtypeStruct((1, m * skip.shape[1]), f32),
+            jax.ShapeDtypeStruct((n,) + starts.shape, jnp.int32),
+        ],
+        scratch_shapes=[
+            pltpu.SemaphoreType.DMA((2,)),
+            pltpu.SemaphoreType.DMA((n,)),
+            pltpu.SemaphoreType.DMA((n,)),
+            pltpu.SemaphoreType.DMA((3, m)),
+            pltpu.SemaphoreType.DMA((3, m)),
+        ],
+        compiler_params=pltpu.CompilerParams(
+            collective_id=1, has_side_effects=True, vmem_limit_bytes=16 << 20
+        ),
+        name="entry",
+    )(source, taps, filt, skip, starts)
 
 
 def reduce_kernel(
@@ -313,11 +435,11 @@
     tok, channels = upstream.shape
     count, me = lax.axis_size("ctx"), lax.axis_index("ctx")
     pairs = lax.axis_size("fsdp")
-    taps = lax.all_gather(short_taps, "fsdp", axis=1, tiled=True)
-    filt = lax.all_gather(long_filter, "fsdp", axis=1, tiled=True)
-    factor = lax.all_gather(skip, "fsdp", axis=0, tiled=True)
-    lists = lax.all_gather(starts[0, 0], "ctx")
-    tail = passed_along(source[tok - 16 :], "ctx", 1)
+    listed = jnp.pad(starts[0], ((0, 7), (0, LANES - starts.shape[2])), constant_values=tok)
+    tail, taps, filt, factor, lists = entry(
+        pairs, count, source, short_taps, long_filter, skip[None], listed
+    )
+    lists = lists[:, 0, : starts.shape[2]]
     places = jnp.arange(count, dtype=jnp.int32)
     positions = jnp.arange(tok, dtype=jnp.int32)
     absolute = jnp.where(lists < tok, lists + (places * tok)[:, None], -FAR)
@@ -332,20 +454,34 @@
 
     last = last_of(me)
     later = jnp.where(me < count - 1, last_of(me + 1) + tok, FAR)
-    last_row = jnp.concatenate([last, later])[None, :]
+    row_turned = jnp.concatenate([later[::-1], last[::-1]])[None, :]
+    last_turned = last[::-1][:, None]
     last = last[:, None]
-    rows = filt.T
-    empty = jnp.zeros_like(rows)
-    ahead = jnp.concatenate([rows[:, ::-1], empty], axis=1)
-    behind = jnp.concatenate([rows, empty], axis=1)
-
-    qf, kf, vf, gate, glin = featurize(last, source, tail, taps, upstream)
-    gate_prev = passed_along(gate, "ctx", 1)
-    glin_next = passed_along(glin, "ctx", -1)
-    mixed, grads, low, edge, short, skip_part, lag = convolve(
-        last, last_row, factor[None], ahead, behind, gate, gate_prev, glin, glin_next,
-        (qf, kf, vf), upstream, source, tail, taps,
-    )
+    ahead = filt[:, ::-1].transpose(0, 2, 1).reshape(-1, LEN)
+
+    chunks = min(CHUNKS, channels // LANES)
+    made = [featurize(c, chunks, last, source, tail, taps, upstream) for c in range(chunks)]
+    moved = [
+        (passed_along(gate, "ctx", 1), passed_along(glin, "ctx", -1))
+        for _, _, _, gate, glin in made
+    ]
+    parts = [
+        convolve(
+            c, chunks, last, last_turned, row_turned, factor, ahead, gate, gate_prev, glin,
+            glin_next, (qf, kf, vf), upstream, source, tail, taps,
+        )
+        for c, ((qf, kf, vf, gate, glin), (gate_prev, glin_next)) in enumerate(zip(made, moved))
+    ]
+    mixed = jnp.concatenate([part[0] for part in parts], axis=1)
+    low, edge, short = (
+        jnp.concatenate([part[i] for part in parts], axis=2).transpose(1, 0, 2).reshape(
+            -1, 3 * channels
+        )
+        for i in (4, 5, 6)
+    )
+    skip_part = jnp.concatenate([part[7] for part in parts], axis=1)
+    lag = jnp.concatenate([part[8] for part in parts], axis=0)
+    grads = jnp.concatenate([part[i] for i in (1, 2, 3) for part in parts], axis=1)
     returned = passed_along(edge[8 - (SHORT - 1) :].astype(jnp.bfloat16), "ctx", -1)
     fixed = low[8 - (SHORT - 1) :] + returned.astype(jnp.float32)
     grads = lax.dynamic_update_slice(grads, fixed.astype(jnp.bfloat16), (tok - (SHORT - 1), 0))

time: 203 us -> 212 us (1.044)
  blocking collectives: 48.3 us -> 0 us
  local copies, waits for them, and re-layouts: 17.8 us -> 65.8 us
  waiting for transfers between devices: 39.3 us -> 0.02 us
  Pallas kernels: 85.5 us -> 105 us
  starting transfers between devices: 9.72 us -> 25.5 us
  other arithmetic: 1.1 us -> 12.6 us
    all_gather x4 -> x0, blocking collectives: 48.3 us -> none  [the longest x1 42.3 us: body(): lists = lax.all_gather(starts[0, 0], 'ctx')]
    unnamed x21 -> x218, local copies, waits for them, and re-layouts: 8.8 us -> 48.2 us
    ppermute x4 -> x9, waiting for transfers between devices: 39.3 us -> 0.02 us  [passed_along(): return lax.ppermute(block, axis, route)]
    ppermute x4 -> x9, starting transfers between devices: 9.72 us -> 25.5 us  [passed_along(): return lax.ppermute(block, axis, route)]
    pallas_call x1 -> x5, Pallas kernels: 56.9 us -> 66.4 us  [the longest x4 48.6 us: convolve(): pl.pallas_call(conv_kernel, grid=(steps,), in_specs=[fixed((tok, 1)), fix...]
    pallas_call x1, Pallas kernels: 18 us -> 24.6 us  [reduced(): pl.pallas_call(functools.partial(reduce_kernel, m, n, scaling), in_specs=...]
    pallas_call x1 -> x4, Pallas kernels: 10.6 us -> 13.6 us  [featurize(): pl.pallas_call(featurize_kernel, grid=(steps,), in_specs=[pl.BlockSpec((t...]
    another operation x0 -> x4, other arithmetic: none -> 2.93 us
  transfers between devices with their start and end apart: 4 -> 9, of which waited for: 2 -> 0; matrix products, arithmetic and copies ran while one was open for 1% -> 8% of each run, Pallas kernels for 9% -> 34%
where the time goes in v2:
time: 212 us; the launch traced here: 210 us
  Pallas kernels  105 us (50%)
  local copies, waits for them, and re-layouts  65.8 us (31%)
  starting transfers between devices  25.5 us (12%)
  other arithmetic  12.6 us (6%)
    pallas_call x4, Pallas kernels, convolve(): pl.pallas_call(conv_kernel, grid=(steps,), in_specs=[fixed((tok, 1)), fix...  48.6 us
    unnamed x218, local copies, waits for them, and re-layouts  48.2 us
    ppermute x9, starting transfers between devices, passed_along(): return lax.ppermute(block, axis, route)  25.5 us
    pallas_call x1, Pallas kernels, reduced(): pl.pallas_call(functools.partial(reduce_kernel, m, n, scaling), in_specs=...  24.6 us
    pallas_call x1, Pallas kernels, entry(): pl.pallas_call(functools.partial(entry_kernel, m, n), in_specs=[pl.BlockS...  17.8 us
    pallas_call x4, Pallas kernels, featurize(): pl.pallas_call(featurize_kernel, grid=(steps,), in_specs=[pl.BlockSpec((t...  13.6 us
  transfers between devices with their start and end apart: 9, of which 0 were waited for; matrix products, arithmetic and copies ran while one was open for 8% of the time, Pallas kernels for 34%

profile of v2, /device:TPU:0, one launch (start us, length us, event | category | flops | bytes accessed | tf_op | source)
XLA Modules:
  0.0 210.3 jit_solution(9704229031049394264)
XLA Ops:
  2.6 1.9 copy-done
  7.6 17.8 %entry.1 = (bf16[16,12288]{1,0:T(8,128)(2,1)S(1)}, f32[7,12288]{1,0:T(8,128)S(1)}, f32[2,128,128]{2,1,0:T(8,128)S(1)}, f32[1,4096]{1,0:T(1,128)S(1)}, s32[16,8,128]{2,1,0:T(8,128)S(1)}) custom-call(bf16[128,12288]{1,0:T(8,128)(2,1)S(1)} %bitcast.44, f32[7,6144]{1,0:T(8,128)S(1)} %copy-done.78, f32[128,128]{1,0:T(8,128)S(1)} %copy-done.93, ...), custom_call_target="tpu_custom_call" | custom-call | tf_op jit(solution)/shard_map/entry/pallas_call | solution.py:309
  27.5 1.3 squeeze.14
  31.2 1.4 copy.41.last
  35.6 3.5 %featurize.7 = (f32[128,1024]{1,0:T(8,128)S(1)}, f32[128,1024]{1,0:T(8,128)S(1)}, f32[128,1024]{1,0:T(8,128)S(1)}, bf16[128,1024]{1,0:T(8,128)(2,1)}, bf16[128,1024]{1,0:T(8,128)(2,1)}) custom-call(s32[128,1]{1,0:T(8,128)S(1)} %copy-done.9, bf16[128,12288]{1,0:T(8,128)(2,1)S(1)} %bitcast.45, bf16[128,12288]{1,0:T(8,128)(2,1)S(1)} %bitcast.46, ...), custom_call_target="tpu_custom_call" | custom-call | tf_op jit(solution)/shard_map/featurize/pallas_call | solution.py:78
  41.5 3.7 %collective-permute-start.6 = (bf16[128,1024]{1,0:T(8,128)(2,1)}, bf16[128,1024]{1,0:T(8,128)(2,1)}, u32[]{:S(2)}, u32[]{:S(2)}) collective-permute-start(bf16[128,1024]{1,0:T(8,128)(2,1)} %get-tuple-element.89.gate), channel_id=1, source_target_pairs={{0,2},{2,4},{4,6},{6,8},{8,10},{10,12},{12,14},{14,16},{16,18},{18... | collective-permute-start | bytes 786440 | tf_op jit(solution)/shard_map/ppermute | solution.py:22
  46.5 3.6 %featurize.6 = (f32[128,1024]{1,0:T(8,128)S(1)}, f32[128,1024]{1,0:T(8,128)S(1)}, f32[128,1024]{1,0:T(8,128)S(1)}, bf16[128,1024]{1,0:T(8,128)(2,1)}, bf16[128,1024]{1,0:T(8,128)(2,1)}) custom-call(s32[128,1]{1,0:T(8,128)S(1)} %copy-done.9, bf16[128,12288]{1,0:T(8,128)(2,1)S(1)} %bitcast.48, bf16[128,12288]{1,0:T(8,128)(2,1)S(1)} %bitcast.49, ...), custom_call_target="tpu_custom_call" | custom-call | tf_op jit(solution)/shard_map/featurize/pallas_call | solution.py:78
  52.6 5.3 %collective-permute-start.4 = (bf16[128,1024]{1,0:T(8,128)(2,1)}, bf16[128,1024]{1,0:T(8,128)(2,1)}, u32[]{:S(2)}, u32[]{:S(2)}) collective-permute-start(bf16[128,1024]{1,0:T(8,128)(2,1)} %get-tuple-element.83.gate), channel_id=1, source_target_pairs={{0,2},{2,4},{4,6},{6,8},{8,10},{10,12},{12,14},{14,16},{16,18},{18... | collective-permute-start | bytes 786440 | tf_op jit(solution)/shard_map/ppermute | solution.py:22
  59.2 3.5 %featurize.5 = (f32[128,1024]{1,0:T(8,128)S(1)}, f32[128,1024]{1,0:T(8,128)S(1)}, f32[128,1024]{1,0:T(8,128)S(1)}, bf16[128,1024]{1,0:T(8,128)(2,1)}, bf16[128,1024]{1,0:T(8,128)(2,1)S(1)}) custom-call(s32[128,1]{1,0:T(8,128)S(1)} %copy-done.9, bf16[128,12288]{1,0:T(8,128)(2,1)S(1)} %bitcast.51, bf16[128,12288]{1,0:T(8,128)(2,1)S(1)} %bitcast.52, ...), custom_call_target="tpu_custom_call" | custom-call | tf_op jit(solution)/shard_map/featurize/pallas_call | solution.py:78
  65.9 5.2 %collective-permute-start.2 = (bf16[128,1024]{1,0:T(8,128)(2,1)}, bf16[128,1024]{1,0:T(8,128)(2,1)}, u32[]{:S(2)}, u32[]{:S(2)}) collective-permute-start(bf16[128,1024]{1,0:T(8,128)(2,1)} %get-tuple-element.77.gate), channel_id=1, source_target_pairs={{0,2},{2,4},{4,6},{6,8},{8,10},{10,12},{12,14},{14,16},{16,18},{18... | collective-permute-start | bytes 786440 | tf_op jit(solution)/shard_map/ppermute | solution.py:22
  75.5 2.9 %featurize.4 = (f32[128,1024]{1,0:T(8,128)S(1)}, f32[128,1024]{1,0:T(8,128)S(1)}, f32[128,1024]{1,0:T(8,128)S(1)}, bf16[128,1024]{1,0:T(8,128)(2,1)S(1)}, bf16[128,1024]{1,0:T(8,128)(2,1)S(1)}) custom-call(s32[128,1]{1,0:T(8,128)S(1)} %copy-done.10, bf16[128,12288]{1,0:T(8,128)(2,1)S(1)} %bitcast.56, bf16[128,12288]{1,0:T(8,128)(2,1)S(1)} %bitcast.55, ...), custom_call_target="tpu_custom_call" | custom-call | tf_op jit(solution)/shard_map/featurize/pallas_call | solution.py:78
  85.7 1.4 copy.42.last_turned
  87.1 1.5 rev.15
  88.6 1.7 copy.39
  92.8 4.6 %collective-permute-start = (bf16[128,1024]{1,0:T(8,128)(2,1)}, bf16[128,1024]{1,0:T(8,128)(2,1)S(1)}, u32[]{:S(2)}, u32[]{:S(2)}) collective-permute-start(bf16[128,1024]{1,0:T(8,128)(2,1)} %copy-done.40), channel_id=1, source_target_pairs={{0,2},{2,4},{4,6},{6,8},{8,10},{10,12},{12,14},{14,16},{16,18},{18... | collective-permute-start | bytes 786440 | tf_op jit(solution)/shard_map/ppermute | solution.py:22
  105.4 12.3 %convolve.7 = (bf16[128,1024]{1,0:T(8,128)(2,1)S(1)}, bf16[128,1024]{1,0:T(8,128)(2,1)S(1)}, bf16[128,1024]{1,0:T(8,128)(2,1)S(1)}, bf16[128,1024]{1,0:T(8,128)(...) custom-call(s32[128,1]{1,0:T(8,128)S(1)} %copy-done.11, ...), custom_call_target="tpu_custom_call" | custom-call | flops 1610612736 | bytes 2883584 | tf_op jit(solution)/shard_map/convolve/pallas_call | solution.py:194
  121.8 1.5 collective-permute-start.1
  123.3 12.2 %convolve.6 = (bf16[128,1024]{1,0:T(8,128)(2,1)S(1)}, bf16[128,1024]{1,0:T(8,128)(2,1)S(1)}, bf16[128,1024]{1,0:T(8,128)(2,1)S(1)}, bf16[128,1024]{1,0:T(8,128)(...) custom-call(s32[128,1]{1,0:T(8,128)S(1)} %copy-done.11, ...), custom_call_target="tpu_custom_call" | custom-call | flops 1610612736 | bytes 2883584 | tf_op jit(solution)/shard_map/convolve/pallas_call | solution.py:194
  139.8 12.3 %convolve.5 = (bf16[128,1024]{1,0:T(8,128)(2,1)S(1)}, bf16[128,1024]{1,0:T(8,128)(2,1)S(1)}, bf16[128,1024]{1,0:T(8,128)(2,1)S(1)}, bf16[128,1024]{1,0:T(8,128)(...) custom-call(s32[128,1]{1,0:T(8,128)S(1)} %copy-done.11, ...), custom_call_target="tpu_custom_call" | custom-call | flops 1610612736 | bytes 2883584 | tf_op jit(solution)/shard_map/convolve/pallas_call | solution.py:194
  153.6 11.8 %convolve.4 = (bf16[128,1024]{1,0:T(8,128)(2,1)S(1)}, bf16[128,1024]{1,0:T(8,128)(2,1)S(1)}, bf16[128,1024]{1,0:T(8,128)(2,1)S(1)}, bf16[128,1024]{1,0:T(8,128)(...) custom-call(s32[128,1]{1,0:T(8,128)S(1)} %copy-done.11, ...), custom_call_target="tpu_custom_call" | custom-call | flops 1610612736 | bytes 2883584 | tf_op jit(solution)/shard_map/convolve/pallas_call | solution.py:194
  175.6 1.4 collective-permute-start.8
  178.9 1.6 copy-done.100
  180.5 24.6 %reduce.9 = f32[16,32,128]{2,1,0:T(8,128)S(1)} custom-call(f32[2,16,32,128]{3,2,1,0:T(8,128)S(1)} %bitcast.81), custom_call_target="tpu_custom_call" | custom-call | tf_op jit(solution)/shard_map/reduce/pallas_call | solution.py:409
  207.9 2.3 %dynamic_update_slice.4 = bf16[1,128,12288]{2,1,0:T(8,128)(2,1)} dynamic-update-slice(bf16[1,128,12288]{2,1,0:T(8,128)(2,1)} %bitcast.98, bf16[1,6,12288]{2,1,0:T(8,128)(2,1)S(1)} %fusion.1, s32[]{:T(128)} %constant.10.clone.1, s32[]{:T(128)} %constant.26.clone.1, s32[]{:T(128)} %constant.10.clone.1) | dynamic-update-slice | bytes 294916 | tf_op jit(solution)/shard_map/dynamic_update_slice | solution.py:487
  (265 shorter events, 69.3 us)
Async XLA Ops:
  7.6 24.9 %copy-start.1 = (bf16[1,128,12288]{2,1,0:T(8,128)(2,1)S(1)}, bf16[1,128,12288]{2,1,0:T(8,128)(2,1)}, u32[]{:S(2)}) copy-start(bf16[1,128,12288]{2,1,0:T(8,128)(2,1)} %param.6) | copy-start | bytes 9437188
  41.5 50.0 %collective-permute-start.6 = (bf16[128,1024]{1,0:T(8,128)(2,1)}, bf16[128,1024]{1,0:T(8,128)(2,1)}, u32[]{:S(2)}, u32[]{:S(2)}) collective-permute-start(bf16[128,1024]{1,0:T(8,128)(2,1)} %get-tuple-element.89.gate), channel_id=1, source_target_pairs={{0,2},{2,4},{4,6},{6,8},{8,10},{10,12},{12,14},{14,16},{16,18},{18... | collective-permute-start | bytes 786440 | tf_op jit(solution)/shard_map/ppermute | solution.py:22
  45.2 47.6 %collective-permute-start.7 = (bf16[128,1024]{1,0:T(8,128)(2,1)}, bf16[128,1024]{1,0:T(8,128)(2,1)}, u32[]{:S(2)}, u32[]{:S(2)}) collective-permute-start(bf16[128,1024]{1,0:T(8,128)(2,1)} %get-tuple-element.90.glin), channel_id=1, source_target_pairs={{2,0},{4,2},{6,4},{8,6},{10,8},{12,10},{14,12},{16,14},{18,16},{20... | collective-permute-start | bytes 786440 | tf_op jit(solution)/shard_map/ppermute | solution.py:22
  52.6 69.1 %collective-permute-start.4 = (bf16[128,1024]{1,0:T(8,128)(2,1)}, bf16[128,1024]{1,0:T(8,128)(2,1)}, u32[]{:S(2)}, u32[]{:S(2)}) collective-permute-start(bf16[128,1024]{1,0:T(8,128)(2,1)} %get-tuple-element.83.gate), channel_id=1, source_target_pairs={{0,2},{2,4},{4,6},{6,8},{8,10},{10,12},{12,14},{14,16},{16,18},{18... | collective-permute-start | bytes 786440 | tf_op jit(solution)/shard_map/ppermute | solution.py:22
  57.9 65.3 %collective-permute-start.5 = (bf16[128,1024]{1,0:T(8,128)(2,1)}, bf16[128,1024]{1,0:T(8,128)(2,1)}, u32[]{:S(2)}, u32[]{:S(2)}) collective-permute-start(bf16[128,1024]{1,0:T(8,128)(2,1)} %get-tuple-element.84.glin), channel_id=1, source_target_pairs={{2,0},{4,2},{6,4},{8,6},{10,8},{12,10},{14,12},{16,14},{18,16},{20... | collective-permute-start | bytes 786440 | tf_op jit(solution)/shard_map/ppermute | solution.py:22
  65.9 73.9 %collective-permute-start.2 = (bf16[128,1024]{1,0:T(8,128)(2,1)}, bf16[128,1024]{1,0:T(8,128)(2,1)}, u32[]{:S(2)}, u32[]{:S(2)}) collective-permute-start(bf16[128,1024]{1,0:T(8,128)(2,1)} %get-tuple-element.77.gate), channel_id=1, source_target_pairs={{0,2},{2,4},{4,6},{6,8},{8,10},{10,12},{12,14},{14,16},{16,18},{18... | collective-permute-start | bytes 786440 | tf_op jit(solution)/shard_map/ppermute | solution.py:22
  91.5 48.2 %collective-permute-start.3 = (bf16[128,1024]{1,0:T(8,128)(2,1)}, bf16[128,1024]{1,0:T(8,128)(2,1)S(1)}, u32[]{:S(2)}, u32[]{:S(2)}) collective-permute-start(bf16[128,1024]{1,0:T(8,128)(2,1)} %copy-done.44), channel_id=1, source_target_pairs={{2,0},{4,2},{6,4},{8,6},{10,8},{12,10},{14,12},{16,14},{18,16},{20... | collective-permute-start | bytes 786440 | tf_op jit(solution)/shard_map/ppermute | solution.py:22
  92.8 60.7 %collective-permute-start = (bf16[128,1024]{1,0:T(8,128)(2,1)}, bf16[128,1024]{1,0:T(8,128)(2,1)S(1)}, u32[]{:S(2)}, u32[]{:S(2)}) collective-permute-start(bf16[128,1024]{1,0:T(8,128)(2,1)} %copy-done.40), channel_id=1, source_target_pairs={{0,2},{2,4},{4,6},{6,8},{8,10},{10,12},{12,14},{14,16},{16,18},{18... | collective-permute-start | bytes 786440 | tf_op jit(solution)/shard_map/ppermute | solution.py:22
  105.3 16.4 %copy-start.43 = (bf16[128,1024]{1,0:T(8,128)(2,1)S(1)}, bf16[128,1024]{1,0:T(8,128)(2,1)}, u32[]{:S(2)}) copy-start(bf16[128,1024]{1,0:T(8,128)(2,1)} %copy-done.42) | copy-start | bytes 786436
  105.3 17.9 %copy-start.13 = (f32[2,128,128]{2,1,0:T(8,128)S(1)}, f32[2,128,128]{2,1,0:T(8,128)}, u32[]{:S(2)}) copy-start(f32[2,128,128]{2,1,0:T(8,128)} %copy.39) | copy-start | bytes 393220
  105.3 17.9 %copy-start.15 = (s32[128,1]{1,0:T(8,128)S(1)}, s32[128,1]{1,0:T(8,128)}, u32[]{:S(2)}) copy-start(s32[128,1]{1,0:T(8,128)} %copy.42.last_turned) | copy-start | bytes 1540
  105.3 17.9 %copy-start.29 = (f32[128,1024]{1,0:T(8,128)S(1)}, f32[128,1024]{1,0:T(8,128)}, u32[]{:S(2)}) copy-start(f32[128,1024]{1,0:T(8,128)} %copy-done.28) | copy-start | bytes 1572868
  105.3 17.9 %copy-start.31 = (f32[128,1024]{1,0:T(8,128)S(1)}, f32[128,1024]{1,0:T(8,128)}, u32[]{:S(2)}) copy-start(f32[128,1024]{1,0:T(8,128)} %copy-done.30) | copy-start | bytes 1572868
  105.4 17.9 %copy-start.33 = (f32[128,1024]{1,0:T(8,128)S(1)}, f32[128,1024]{1,0:T(8,128)}, u32[]{:S(2)}) copy-start(f32[128,1024]{1,0:T(8,128)} %copy-done.32) | copy-start | bytes 1572868
  121.8 31.8 %collective-permute-start.1 = (bf16[128,1024]{1,0:T(8,128)(2,1)S(1)}, bf16[128,1024]{1,0:T(8,128)(2,1)S(1)}, u32[]{:S(2)}, u32[]{:S(2)}) collective-permute-start(bf16[128,1024]{1,0:T(8,128)(2,1)S(1)} %copy-done.43), channel_id=1, source_target_pairs={{2,0},{4,2},{6,4},{8,6},{10,8},{12,10},{14,12},{16,14},{18,16},{20... | collective-permute-start | bytes 786440 | tf_op jit(solution)/shard_map/ppermute | solution.py:22
  123.3 16.4 %copy-start.23 = (f32[128,1024]{1,0:T(8,128)S(1)}, f32[128,1024]{1,0:T(8,128)}, u32[]{:S(2)}) copy-start(f32[128,1024]{1,0:T(8,128)} %copy-done.22) | copy-start | bytes 1572868
  123.3 16.4 %copy-start.25 = (f32[128,1024]{1,0:T(8,128)S(1)}, f32[128,1024]{1,0:T(8,128)}, u32[]{:S(2)}) copy-start(f32[128,1024]{1,0:T(8,128)} %copy-done.24) | copy-start | bytes 1572868
  123.3 16.4 %copy-start.27 = (f32[128,1024]{1,0:T(8,128)S(1)}, f32[128,1024]{1,0:T(8,128)}, u32[]{:S(2)}) copy-start(f32[128,1024]{1,0:T(8,128)} %copy-done.26) | copy-start | bytes 1572868
  123.3 16.4 %copy-start.45 = (bf16[128,1024]{1,0:T(8,128)(2,1)S(1)}, bf16[128,1024]{1,0:T(8,128)(2,1)}, u32[]{:S(2)}) copy-start(bf16[128,1024]{1,0:T(8,128)(2,1)} %copy-done.44) | copy-start | bytes 786436
  139.8 13.8 %copy-start.17 = (f32[128,1024]{1,0:T(8,128)S(1)}, f32[128,1024]{1,0:T(8,128)}, u32[]{:S(2)}) copy-start(f32[128,1024]{1,0:T(8,128)} %copy-done.16) | copy-start | bytes 1572868
  139.8 13.8 %copy-start.19 = (f32[128,1024]{1,0:T(8,128)S(1)}, f32[128,1024]{1,0:T(8,128)}, u32[]{:S(2)}) copy-start(f32[128,1024]{1,0:T(8,128)} %copy-done.18) | copy-start | bytes 1572868
  139.8 13.8 %copy-start.21 = (f32[128,1024]{1,0:T(8,128)S(1)}, f32[128,1024]{1,0:T(8,128)}, u32[]{:S(2)}) copy-start(f32[128,1024]{1,0:T(8,128)} %copy-done.20) | copy-start | bytes 1572868
  175.6 32.3 %collective-permute-start.8 = (bf16[6,12288]{1,0:T(8,128)(2,1)S(1)}, bf16[6,12288]{1,0:T(8,128)(2,1)S(1)}, u32[]{:S(2)}, u32[]{:S(2)}) collective-permute-start(bf16[6,12288]{1,0:T(8,128)(2,1)S(1)} %bitcast.97), channel_id=1, source_target_pairs={{2,0},{4,2},{6,4},{8,6},{10,8},{12,10},{14,12},{16,14},{18,16},{20... | collective-permute-start | bytes 442376 | tf_op jit(solution)/shard_map/ppermute | solution.py:22
  177.7 29.5 %copy-start.47 = (bf16[128,1024]{1,0:T(8,128)(2,1)S(1)}, bf16[128,1024]{1,0:T(8,128)(2,1)}, u32[]{:S(2)}) copy-start(bf16[128,1024]{1,0:T(8,128)(2,1)} %copy-done.46) | copy-start | bytes 786436
  (87 other events, 226.2 us)

commit v3 on v2

v3 whole, which is shorter than its diff:
```python
import functools

import jax
import jax.numpy as jnp
from jax import lax
from jax.experimental import pallas as pl
from jax.experimental.pallas import tpu as pltpu
from jax.sharding import PartitionSpec as P

GROUP = 16
LEN = 128
SHORT = 7
LANES = 128
FAR = 1 << 29
MESH = pl.DeviceIdType.MESH


def passed_along(block, axis, distance):
    devices = range(lax.axis_size(axis))
    route = [(i - distance, i) for i in devices if i - distance in devices]
    return lax.ppermute(block, axis, route)


def exchange_matrix(size):
    r = lax.broadcasted_iota(jnp.int32, (size, size), 0)
    c = lax.broadcasted_iota(jnp.int32, (size, size), 1)
    return (r + c == size - 1).astype(jnp.bfloat16)


def operator_kernel(
    n, per, last, last_turned, row_turned, skip, ahead, proj, tail, taps, up,
    mixed, grads, low, edge, short, skip_out, lag,
    feats, gate, glin, gate_prev, glin_next, pad, spill, tiles_f, tiles_b, picked,
    gate_send, gate_recv, glin_send, glin_recv,
):
    me, half = lax.axis_index("ctx"), lax.axis_index("fsdp")
    right, left = lax.rem(me + 1, n), lax.rem(me + n - 1, n)
    blocks, tok = gate.shape[0], gate.shape[1]
    chunks, count = blocks // per, LANES // GROUP
    f32, bf16 = jnp.float32, jnp.bfloat16
    barrier = pltpu.get_barrier_semaphore()
    for to in (left, right):
        pl.semaphore_signal(barrier, inc=1, device_id=(to, half), device_id_type=MESH)
    pl.semaphore_wait(barrier, 2)
    rows = lax.broadcasted_iota(jnp.int32, (tok, LANES), 0)
    cols = lax.broadcasted_iota(jnp.int32, (tok, LANES), 1)
    spill[:, 0:8, :] = jnp.zeros((SHORT, 8, LANES), f32)
    spill[:, tok + 8 :, :] = jnp.zeros((SHORT, 8, LANES), f32)

    def lanes(block, part=0):
        return pl.ds(pl.multiple_of((part * blocks + block) * LANES, LANES), LANES)

    def copies(chunk):
        at = pl.ds(chunk * per, per)
        return (
            pltpu.make_async_remote_copy(
                src_ref=gate.at[at], dst_ref=gate_prev.at[at], send_sem=gate_send.at[chunk],
                recv_sem=gate_recv.at[chunk], device_id=(right, half), device_id_type=MESH,
            ),
            pltpu.make_async_remote_copy(
                src_ref=glin.at[at], dst_ref=glin_next.at[at], send_sem=glin_send.at[chunk],
                recv_sem=glin_recv.at[chunk], device_id=(left, half), device_id_type=MESH,
            ),
        )

    def load_rows(block):
        for part in range(3):
            at = lanes(block, part)
            pad[part, 0:8, :] = tail[:, at].astype(f32)[8:16]
            pad[part, 8:, :] = proj[:, at].astype(f32)

    def earlier(part, offset):
        return pad[part, 8 - offset : 8 - offset + tok, :]

    def featurize(block, carry):
        load_rows(block)
        made = []
        for part in range(3):
            at = lanes(block, part)
            total = jnp.zeros((tok, LANES), f32)
            for offset in range(SHORT):
                kept = jnp.where(last[...] <= rows - offset, earlier(part, offset), 0.0)
                total = total + taps[offset : offset + 1, at] * kept
            feats[part, block] = total
            made.append(total)
        gate[block] = (made[1] * made[2]).astype(bf16)
        through = (up[:, lanes(block)].astype(f32) * made[0]).astype(bf16)
        turned = jnp.dot(exchange_matrix(tok), through, preferred_element_type=f32)
        glin[block] = turned.astype(bf16)
        return carry

    def prepare(chunk, carry):
        lax.fori_loop(chunk * per, (chunk + 1) * per, featurize, 0)
        for copy in copies(chunk):
            copy.start()
        return carry

    lax.fori_loop(0, chunks, prepare, 0)

    def convolve(block, carry):
        at = lanes(block)
        start = last[...]
        start_turned = last_turned[...]
        below = cols <= rows
        fwd_prev = jnp.logical_and(cols > rows, start <= cols - tok)
        fwd_own = jnp.logical_and(below, start <= cols)
        turned = tok - 1 - rows
        bwd_next = jnp.logical_and(cols > rows, row_turned[0:1, :tok] <= turned)
        bwd_own = jnp.logical_and(below, row_turned[0:1, tok:] <= turned)
        lag_prev = jnp.logical_and(cols > turned, start_turned <= cols - tok)
        lag_own = jnp.logical_and(cols <= turned, start_turned <= cols)
        lane = cols // GROUP
        own_gate, own_glin = gate[block], glin[block]
        gate_win = jnp.concatenate([gate_prev[block], own_gate], axis=0)
        glin_win = jnp.concatenate([glin_next[block], own_glin], axis=0)
        glin_f = own_glin.astype(f32)
        filters = ahead[pl.ds(pl.multiple_of(block * count, count), count), :]
        for g in range(count):
            part = slice(g * tok, (g + 1) * tok)
            tile = jnp.broadcast_to(filters[g : g + 1, :], (tok, LEN))
            tile = pltpu.roll(tile, 1, 1, stride=1, stride_axis=0)
            tiles_f[part, :tok] = jnp.where(fwd_prev, tile, 0.0).astype(bf16)
            tiles_f[part, tok:] = jnp.where(fwd_own, tile, 0.0).astype(bf16)
            tiles_b[part, :tok] = jnp.where(bwd_next, tile, 0.0).astype(bf16)
            tiles_b[part, tok:] = jnp.where(bwd_own, tile, 0.0).astype(bf16)
            picked[part, :] = jnp.where(lane == g, glin_f, 0.0).astype(bf16)
        out_f = jnp.dot(tiles_f[...], gate_win, preferred_element_type=f32)
        out_b = jnp.dot(tiles_b[...], glin_win, preferred_element_type=f32)
        product = lax.dot_general(
            picked[...], gate_win, (((1,), (1,)), ((), ())), preferred_element_type=f32
        )
        long_out, spread = out_f[:tok], out_b[:tok]
        for g in range(count):
            part = slice(g * tok, (g + 1) * tok)
            if g:
                long_out = jnp.where(lane == g, out_f[part], long_out)
                spread = jnp.where(lane == g, out_b[part], spread)
            folded = jnp.where(lag_prev, product[part, :tok], 0.0)
            folded = jnp.where(lag_own, product[part, tok:], folded)
            folded = pltpu.roll(folded, 0, 1, stride=1, stride_axis=0)
            lag[block, g : g + 1, :] = jnp.sum(folded, axis=0, keepdims=True)
        flip = exchange_matrix(tok)
        high = spread.astype(bf16)
        rest = (spread - high.astype(f32)).astype(bf16)
        spread = jnp.dot(flip, high, preferred_element_type=f32) + jnp.dot(
            flip, rest, preferred_element_type=f32
        )
        gate_f = own_gate.astype(f32)
        query, key, value = feats[0, block], feats[1, block], feats[2, block]
        upstream = up[:, at].astype(f32)
        factor = skip[:, at]
        combined = long_out + factor * gate_f
        mixed[:, at] = (query * combined).astype(bf16)
        through = upstream * query
        skip_out[:, at] = jnp.sum(through * gate_f, axis=0, keepdims=True)
        grad_gate = spread + factor * through
        load_rows(block)
        for part, grad in enumerate((upstream * combined, grad_gate * value, grad_gate * key)):
            at = lanes(block, part)
            for offset in range(SHORT):
                kept = jnp.where(start <= rows - offset, grad, 0.0)
                short[offset : offset + 1, at] = jnp.sum(
                    kept * earlier(part, offset), axis=0, keepdims=True
                )
                spill[offset, 8 : tok + 8, :] = taps[offset : offset + 1, at] * kept
            total = spill[0, 0 : tok + 8, :]
            for offset in range(1, SHORT):
                total = total + spill[offset, offset : offset + tok + 8, :]
            grads[:, at] = total[8:].astype(bf16)
            low[:, at] = total[tok:]
            edge[:, at] = total[:8]
        return carry

    def use(chunk, carry):
        for copy in copies(chunk):
            copy.wait_recv()
        lax.fori_loop(chunk * per, (chunk + 1) * per, convolve, 0)
        return carry

    lax.fori_loop(0, chunks, use, 0)

    def sent(chunk, carry):
        for copy in copies(chunk):
            copy.wait_send()
        return carry

    lax.fori_loop(0, chunks, sent, 0)


def operate(n, last, last_turned, row_turned, skip, ahead, source, tail, taps, upstream):
    tok, channels = upstream.shape
    blocks = channels // LANES
    per = min(4, blocks)
    count = LANES // GROUP
    f32 = jnp.float32
    vmem = pl.BlockSpec(memory_space=pltpu.VMEM)
    half = pltpu.VMEM((blocks, tok, LANES), jnp.bfloat16)
    tiles = pltpu.VMEM((count * tok, 2 * tok), jnp.bfloat16)
    sems = pltpu.SemaphoreType.DMA((blocks // per,))
    return pl.pallas_call(
        functools.partial(operator_kernel, n, per),
        in_specs=[vmem] * 9,
        out_specs=[vmem] * 7,
        out_shape=[
            jax.ShapeDtypeStruct((tok, channels), jnp.bfloat16),
            jax.ShapeDtypeStruct((tok, 3 * channels), jnp.bfloat16),
            jax.ShapeDtypeStruct((8, 3 * channels), f32),
            jax.ShapeDtypeStruct((8, 3 * channels), f32),
            jax.ShapeDtypeStruct((SHORT, 3 * channels), f32),
            jax.ShapeDtypeStruct((1, channels), f32),
            jax.ShapeDtypeStruct((blocks, count, LEN), f32),
        ],
        scratch_shapes=[
            pltpu.VMEM((3, blocks, tok, LANES), f32),
            half,
            half,
            half,
            half,
            pltpu.VMEM((3, tok + 8, LANES), f32),
            pltpu.VMEM((SHORT, tok + 16, LANES), f32),
            tiles,
            tiles,
            pltpu.VMEM((count * tok, LANES), jnp.bfloat16),
            sems,
            sems,
            sems,
            sems,
        ],
        compiler_params=pltpu.CompilerParams(
            collective_id=2, has_side_effects=True, vmem_limit_bytes=48 << 20
        ),
        name="operate",
    )(last, last_turned, row_turned, skip, ahead, source, tail, taps, upstream)


def entry_kernel(m, n, proj, taps, filt, skip, starts, tail, taps_all, filt_all, skip_all,
                 last, last_turned, row_turned, lists, tail_sems, start_send, start_recv, share_send, share_recv):
    me, half = lax.axis_index("ctx"), lax.axis_index("fsdp")
    tok, width, skips = proj.shape[0], taps.shape[1], skip.shape[1]
    barrier = pltpu.get_barrier_semaphore()

    def greet_share(i, carry):
        pl.semaphore_signal(
            barrier, inc=1, device_id=(me, lax.rem(half + i, m)), device_id_type=MESH
        )
        return carry

    def greet(i, carry):
        pl.semaphore_signal(
            barrier, inc=1, device_id=(lax.rem(me + i, n), half), device_id_type=MESH
        )
        return carry

    lax.fori_loop(1, m, greet_share, 0)
    lax.fori_loop(1, n, greet, 0)
    pl.semaphore_wait(barrier, m + n - 2)
    taps_at = pl.ds(pl.multiple_of(half * width, LANES), width)
    skip_at = pl.ds(pl.multiple_of(half * skips, LANES), skips)

    def first(i):
        return pltpu.make_async_remote_copy(
            src_ref=starts, dst_ref=lists.at[me], send_sem=start_send.at[i],
            recv_sem=start_recv.at[i], device_id=(lax.rem(me + i, n), half), device_id_type=MESH,
        )

    def shares(i):
        to = lax.rem(half + i, m)
        pairs = (
            (taps, taps_all.at[:, taps_at]),
            (filt, filt_all.at[half]),
            (skip, skip_all.at[:, skip_at]),
        )
        return [
            pltpu.make_async_remote_copy(
                src_ref=src, dst_ref=dst, send_sem=share_send.at[j, i],
                recv_sem=share_recv.at[j, i], device_id=(me, to), device_id_type=MESH,
            )
            for j, (src, dst) in enumerate(pairs)
        ]

    onward = pltpu.make_async_remote_copy(
        src_ref=proj.at[tok - 16 : tok], dst_ref=tail, send_sem=tail_sems.at[0],
        recv_sem=tail_sems.at[1], device_id=(lax.rem(me + 1, n), half), device_id_type=MESH,
    )
    onward.start()

    def start_first(i, carry):
        first(i).start()
        return carry

    def start_share(i, carry):
        for copy in shares(i):
            copy.start()
        return carry

    def wait_first(i, carry):
        first(i).wait()
        return carry

    def wait_share(i, carry):
        for copy in shares(i):
            copy.wait()
        return carry

    lax.fori_loop(1, n, start_first, 0)
    lax.fori_loop(1, m, start_share, 0)
    lists[me] = starts[...]
    taps_all[:, taps_at] = taps[...]
    filt_all[half] = filt[...]
    skip_all[:, skip_at] = skip[...]
    lax.fori_loop(1, n, wait_first, 0)
    rows = lax.broadcasted_iota(jnp.int32, (tok, LANES), 0)
    cols = lax.broadcasted_iota(jnp.int32, (tok, LANES), 1)

    def latest(places):
        def look(j, best):
            listed = lists[j, 0:1, :]
            placed = jnp.where(listed < tok, listed + (j - me) * tok, -FAR)
            return jnp.maximum(best, jnp.where(placed <= places, placed, -FAR))

        best = lax.fori_loop(0, n, look, jnp.full((tok, LANES), -FAR, jnp.int32))
        top = jnp.max(best.astype(jnp.float32), axis=1, keepdims=True)
        return jnp.broadcast_to(top, (tok, LANES))

    def as_row(column):
        return jnp.sum(jnp.where(rows == cols, column, 0.0), axis=0, keepdims=True)

    own = latest(rows)
    turned = latest(tok - 1 - rows)
    later = latest(2 * tok - 1 - rows)
    last[...] = own.astype(jnp.int32)
    last_turned[...] = turned.astype(jnp.int32)
    later = jnp.where(me < n - 1, as_row(later).astype(jnp.int32), FAR)
    row_turned[:, :tok] = jnp.broadcast_to(later, (8, tok))
    row_turned[:, tok:] = jnp.broadcast_to(as_row(turned).astype(jnp.int32), (8, tok))
    lax.fori_loop(1, m, wait_share, 0)
    onward.wait()


def entry(m, n, source, taps, filt, skip, starts):
    vmem = pl.BlockSpec(memory_space=pltpu.VMEM)
    f32 = jnp.float32
    return pl.pallas_call(
        functools.partial(entry_kernel, m, n),
        in_specs=[pl.BlockSpec(memory_space=pl.ANY)] + [vmem] * 4,
        out_specs=[vmem] * 7,
        out_shape=[
            jax.ShapeDtypeStruct((16, source.shape[1]), source.dtype),
            jax.ShapeDtypeStruct((SHORT, m * taps.shape[1]), f32),
            jax.ShapeDtypeStruct((m,) + filt.shape, f32),
            jax.ShapeDtypeStruct((1, m * skip.shape[1]), f32),
            jax.ShapeDtypeStruct((source.shape[0], LANES), jnp.int32),
            jax.ShapeDtypeStruct((source.shape[0], LANES), jnp.int32),
            jax.ShapeDtypeStruct((8, 2 * source.shape[0]), jnp.int32),
        ],
        scratch_shapes=[
            pltpu.VMEM((n,) + starts.shape, jnp.int32),
            pltpu.SemaphoreType.DMA((2,)),
            pltpu.SemaphoreType.DMA((n,)),
            pltpu.SemaphoreType.DMA((n,)),
            pltpu.SemaphoreType.DMA((3, m)),
            pltpu.SemaphoreType.DMA((3, m)),
        ],
        compiler_params=pltpu.CompilerParams(
            collective_id=1, has_side_effects=True, vmem_limit_bytes=16 << 20
        ),
        name="entry",
    )(source, taps, filt, skip, starts)


def reduce_kernel(
    m, n, scaling, x, out, pair, mine, parts, result, send0, recv0, send1, recv1, send2, recv2
):
    me, half = lax.axis_index("ctx"), lax.axis_index("fsdp")
    barrier = pltpu.get_barrier_semaphore()

    def greet_share(i, carry):
        pl.semaphore_signal(
            barrier, inc=1, device_id=(me, lax.rem(half + i, m)), device_id_type=MESH
        )
        return carry

    def greet(i, carry):
        pl.semaphore_signal(
            barrier, inc=1, device_id=(lax.rem(me + i, n), half), device_id_type=MESH
        )
        return carry

    lax.fori_loop(1, m, greet_share, 0)
    lax.fori_loop(1, n, greet, 0)
    pl.semaphore_wait(barrier, m + n - 2)

    def started(make, stop):
        def run(i, carry):
            make(i).start()
            return carry
        lax.fori_loop(1, stop, run, 0)

    def waited(make, stop):
        def run(i, carry):
            make(i).wait()
            return carry
        lax.fori_loop(1, stop, run, 0)

    def share(i):
        to = lax.rem(half + i, m)
        return pltpu.make_async_remote_copy(
            src_ref=x.at[to], dst_ref=pair.at[i], send_sem=send0.at[i], recv_sem=recv0.at[i],
            device_id=(me, to), device_id_type=MESH,
        )

    started(share, m)
    waited(share, m)
    owned = lax.fori_loop(1, m, lambda i, total: total + pair[i], x[half])
    mine[...] = (owned * scaling).astype(jnp.bfloat16)

    def scatter(i):
        to = lax.rem(me + i, n)
        return pltpu.make_async_remote_copy(
            src_ref=mine.at[to], dst_ref=parts.at[i], send_sem=send1.at[i], recv_sem=recv1.at[i],
            device_id=(to, half), device_id_type=MESH,
        )

    def gather(i):
        return pltpu.make_async_remote_copy(
            src_ref=result.at[me], dst_ref=result.at[me], send_sem=send2.at[i],
            recv_sem=recv2.at[i], device_id=(lax.rem(me + i, n), half), device_id_type=MESH,
        )

    started(scatter, n)
    waited(scatter, n)

    def add(i, total):
        return total + parts[i].astype(jnp.float32)

    total = lax.fori_loop(1, n, add, mine[me].astype(jnp.float32))
    result[me] = total.astype(jnp.bfloat16)
    started(gather, n)
    waited(gather, n)
    out[...] = result[...].astype(jnp.float32)


def reduced(packed, scaling):
    m, n, rows, _ = packed.shape
    half = pltpu.VMEM((n, rows, LANES), jnp.bfloat16)
    return pl.pallas_call(
        functools.partial(reduce_kernel, m, n, scaling),
        in_specs=[pl.BlockSpec(memory_space=pltpu.VMEM)],
        out_specs=pl.BlockSpec(memory_space=pltpu.VMEM),
        out_shape=jax.ShapeDtypeStruct((n, rows, LANES), jnp.float32),
        scratch_shapes=[
            pltpu.VMEM((m, n, rows, LANES), jnp.float32),
            half,
            half,
            half,
            pltpu.SemaphoreType.DMA((m,)),
            pltpu.SemaphoreType.DMA((m,)),
            pltpu.SemaphoreType.DMA((n,)),
            pltpu.SemaphoreType.DMA((n,)),
            pltpu.SemaphoreType.DMA((n,)),
            pltpu.SemaphoreType.DMA((n,)),
        ],
        compiler_params=pltpu.CompilerParams(
            collective_id=0, has_side_effects=True, vmem_limit_bytes=32 << 20
        ),
        name="reduce",
    )(packed)


def body(proj, short_taps, long_filter, skip, grad_out, starts):
    source, upstream = proj[0], grad_out[0]
    tok, channels = upstream.shape
    count = lax.axis_size("ctx")
    pairs = lax.axis_size("fsdp")
    listed = jnp.pad(starts[0], ((0, 7), (0, LANES - starts.shape[2])), constant_values=tok)
    tail, taps, filt, factor, last, last_turned, row_turned = entry(
        pairs, count, source, short_taps, long_filter, skip[None], listed
    )
    ahead = filt[:, ::-1].transpose(0, 2, 1).reshape(-1, LEN)
    mixed, grads, low, edge, short, skip_part, lag = operate(
        count, last, last_turned, row_turned, factor, ahead, source, tail, taps, upstream
    )
    lag = lag.reshape(-1, LEN)
    returned = passed_along(edge[8 - (SHORT - 1) :].astype(jnp.bfloat16), "ctx", -1)
    fixed = low[8 - (SHORT - 1) :] + returned.astype(jnp.float32)
    grads = lax.dynamic_update_slice(grads, fixed.astype(jnp.bfloat16), (tok - (SHORT - 1), 0))

    scaling = float(pairs * count * tok) ** (-0.5)
    own = 3 * channels // pairs
    groups = channels // GROUP
    long_grad = lag[:, ::-1].T
    sizes = (SHORT * own, LEN * (groups // pairs), channels // pairs)
    flat = jnp.concatenate(
        [
            short.reshape(SHORT, pairs, own).transpose(1, 0, 2).reshape(pairs, -1),
            long_grad.reshape(LEN, pairs, groups // pairs).transpose(1, 0, 2).reshape(pairs, -1),
            skip_part.reshape(pairs, -1),
        ],
        axis=1,
    )
    unit = count * 16 * LANES
    padded = -(-flat.shape[1] // unit) * unit
    flat = jnp.pad(flat, ((0, 0), (0, padded - flat.shape[1])))
    summed = reduced(flat.reshape(pairs, count, -1, LANES), scaling).reshape(-1)
    a, b, c = sizes
    return (
        mixed[None],
        grads[None],
        summed[:a].reshape(SHORT, own),
        summed[a : a + b].reshape(LEN, groups // pairs),
        summed[a + b : a + b + c],
    )


def solution(mesh):
    window = P("fsdp", "ctx", None)
    return jax.shard_map(
        body,
        mesh=mesh,
        in_specs=(window, P(None, "fsdp"), P(None, "fsdp"), P("fsdp"), window, window),
        out_specs=(window, window, P(None, "fsdp"), P(None, "fsdp"), P("fsdp")),
        check_vma=False,
    )
```

time: 212 us -> 135 us (0.64)
  local copies, waits for them, and re-layouts: 65.8 us -> 21.9 us
  starting transfers between devices: 25.5 us -> 1.28 us
  other arithmetic: 12.6 us -> 1.69 us
  Pallas kernels: 105 us -> 109 us
    unnamed x218 -> x30, local copies, waits for them, and re-layouts: 48.2 us -> 14.7 us
    ppermute x9 -> x1, starting transfers between devices: 25.5 us -> 1.28 us  [passed_along(): return lax.ppermute(block, axis, route)]
    pallas_call x1, Pallas kernels: 24.6 us -> 31.7 us  [reduced(): pl.pallas_call(functools.partial(reduce_kernel, m, n, scaling), in_specs=...]
    pallas_call x8 -> x1, Pallas kernels: 62.2 us -> 58.1 us  [operate(): pl.pallas_call(functools.partial(operator_kernel, n, per), in_specs=[vmem...]
    another operation x4 -> x0, other arithmetic: 2.93 us -> none
    concatenate x4 -> x0, other arithmetic: 2.71 us -> none  [the longest x1 1.12 us: body(): jnp.concatenate([part[i] for part in parts], axis=2).transpose(1, 0, 2)]
    broadcast_in_dim x2 -> x0, other arithmetic: 2.19 us -> none  [the longest x1 1.14 us: body(): last_turned = last[::-1][:, None]]
  transfers between devices with their start and end apart: 9 -> 1, of which waited for: 0 -> 0; matrix products, arithmetic and copies ran while one was open for 8% -> 4% of each run, Pallas kernels for 34% -> 24%
where the time goes in v3:
time: 135 us; the launch traced here: 134 us
  Pallas kernels  109 us (81%)
  local copies, waits for them, and re-layouts  21.9 us (16%)
  other arithmetic  1.69 us (1%)
    pallas_call x1, Pallas kernels, operate(): pl.pallas_call(functools.partial(operator_kernel, n, per), in_specs=[vmem...  58.1 us
    pallas_call x1, Pallas kernels, reduced(): pl.pallas_call(functools.partial(reduce_kernel, m, n, scaling), in_specs=...  31.7 us
    pallas_call x1, Pallas kernels, entry(): pl.pallas_call(functools.partial(entry_kernel, m, n), in_specs=[pl.BlockS...  18.9 us
    unnamed x30, local copies, waits for them, and re-layouts  14.7 us
  transfers between devices with their start and end apart: 1, of which 0 were waited for; matrix products, arithmetic and copies ran while one was open for 4% of the time, Pallas kernels for 24%

profile of v3, /device:TPU:0, one launch (start us, length us, event | category | flops | bytes accessed | tf_op | source)
XLA Modules:
  0.0 134.3 jit_solution(7217742259746035952)
XLA Ops:
  0.6 0.7 pad.8.starts
  1.3 1.9 %copy-done = bf16[1,128,12288]{2,1,0:T(8,128)(2,1)S(1)} copy-done((bf16[1,128,12288]{2,1,0:T(8,128)(2,1)S(1)}, bf16[1,128,12288]{2,1,0:T(8,128)(2,1)}, u32[]{:S(2)}) %copy-start) | copy-done | bytes 3145752
  3.2 0.9 copy-done.3
  4.1 0.8 copy-done.8
  5.0 0.7 copy-done.10
  5.6 18.9 %entry.1 = (bf16[16,12288]{1,0:T(8,128)(2,1)S(1)}, f32[7,12288]{1,0:T(8,128)S(1)}, f32[2,128,128]{2,1,0:T(8,128)S(1)}, f32[1,4096]{1,0:T(1,128)S(1)}, s32[128,12...) custom-call(bf16[128,12288]{1,0:T(8,128)(2,1)S(1)} %bitcast.29, f32[7,6144]{1,0:T(8,128)S(1)} %copy-done.3, ...), custom_call_target="tpu_custom_call" | custom-call | tf_op jit(solution)/shard_map/entry/pallas_call | solution.py:343
  24.6 0.6 copy-done.4
  25.2 0.6 copy-done.6
  26.4 0.8 copy-done.5
  27.3 0.8 copy-done.7
  28.1 0.7 copy-done.12
  28.8 58.1 %operate.1 = (bf16[128,4096]{1,0:T(8,128)(2,1)S(1)}, bf16[128,12288]{1,0:T(8,128)(2,1)}, f32[8,12288]{1,0:T(8,128)S(1)}, f32[8,12288]{1,0:T(8,128)S(1)}, f32[7,1...) custom-call(s32[128,128]{1,0:T(8,128)S(1)} %copy-done.5, s32[128,128]{1,0:T(8,128)S(1)} %copy-done.7, ...), custom_call_target="tpu_custom_call" | custom-call | tf_op jit(solution)/shard_map/operate/pallas_call | solution.py:200
  86.9 0.7 copy-done.2
  87.7 0.6 copy-done.9
  88.3 1.3 collective-permute-start
  90.0 1.3 reshape.46
  91.8 1.4 %reduce.4 = f32[4096]{0:T(1024)S(1)} reduce(f32[1,4096]{1,0:T(1,128)} %copy-done.9, f32[]{:T(128)} %broadcast.15), dimensions={0}, to_apply=%get-tuple-element.32.reduce_sub_computation.3 | reduce | bytes 32772 | tf_op jit(solution)/shard_map/operate/pallas_call | solution.py:200
  93.5 31.7 %reduce.5 = f32[16,32,128]{2,1,0:T(8,128)S(1)} custom-call(f32[2,16,32,128]{3,2,1,0:T(8,128)S(1)} %bitcast.30), custom_call_target="tpu_custom_call" | custom-call | tf_op jit(solution)/shard_map/reduce/pallas_call | solution.py:446
  125.2 0.6 slice.28
  125.8 0.7 reshape.54
  126.6 0.6 slice.27
  127.3 2.2 %dynamic_update_slice.4 = bf16[1,128,12288]{2,1,0:T(8,128)(2,1)} dynamic-update-slice(bf16[1,128,12288]{2,1,0:T(8,128)(2,1)} %bitcast.39, bf16[1,6,12288]{2,1,0:T(8,128)(2,1)S(1)} %fusion.1, s32[]{:T(128)} %constant.6.clone.1, s32[]{:T(128)} %constant.7.clone.1, s32[]{:T(128)} %constant.6.clone.1) | dynamic-update-slice | bytes 294916 | tf_op jit(solution)/shard_map/dynamic_update_slice | solution.py:486
  129.5 1.0 copy.20
  130.5 3.8 %copy.21 = bf16[1,128,12288]{2,1,0:T(8,128)(2,1)} copy(bf16[1,128,12288]{2,1,0:T(8,128)(2,1)} %dynamic_update_slice.4) | data formatting | bytes 6291456
  (28 shorter events, 1.9 us)
Async XLA Ops:
  1.3 1.9 %copy-start = (bf16[1,128,12288]{2,1,0:T(8,128)(2,1)S(1)}, bf16[1,128,12288]{2,1,0:T(8,128)(2,1)}, u32[]{:S(2)}) copy-start(bf16[1,128,12288]{2,1,0:T(8,128)(2,1)} %param.6) | copy-start | bytes 9437188
  3.2 0.9 copy-start.3
  4.1 0.8 copy-start.8
  5.0 0.7 copy-start.10
  5.6 20.8 %copy-start.1 = (bf16[1,128,4096]{2,1,0:T(8,128)(2,1)S(1)}, bf16[1,128,4096]{2,1,0:T(8,128)(2,1)}, u32[]{:S(2)}) copy-start(bf16[1,128,4096]{2,1,0:T(8,128)(2,1)} %param.10) | copy-start | bytes 3145732
  24.5 0.6 copy-start.4
  25.2 0.6 copy-start.6
  25.8 0.6 copy-start.11
  26.4 0.8 copy-start.5
  27.3 0.8 copy-start.7
  28.1 0.7 copy-start.12
  86.9 0.7 copy-start.2
  87.7 0.6 copy-start.9
  88.3 38.9 %collective-permute-start = (bf16[6,12288]{1,0:T(8,128)(2,1)S(1)}, bf16[6,12288]{1,0:T(8,128)(2,1)S(1)}, u32[]{:S(2)}, u32[]{:S(2)}) collective-permute-start(bf16[6,12288]{1,0:T(8,128)(2,1)S(1)} %slice.33), channel_id=1, source_target_pairs={{2,0},{4,2},{6,4},{8,6},{10,8},{12,10},{14,12},{16,14},{18,16},{20... | collective-permute-start | bytes 442376 | tf_op jit(solution)/shard_map/ppermute | solution.py:21

commit v4 on v3

v4 whole, which is shorter than its diff:
```python
import functools

import jax
import jax.numpy as jnp
from jax import lax
from jax.experimental import pallas as pl
from jax.experimental.pallas import tpu as pltpu
from jax.sharding import PartitionSpec as P

GROUP = 16
LEN = 128
SHORT = 7
LANES = 128
FAR = 1 << 29
MESH = pl.DeviceIdType.MESH


def exchange_matrix(size):
    r = lax.broadcasted_iota(jnp.int32, (size, size), 0)
    c = lax.broadcasted_iota(jnp.int32, (size, size), 1)
    return (r + c == size - 1).astype(jnp.bfloat16)


def operator_kernel(
    m, n, per, scaling, proj, up, taps_own, filt_own, skip_own, starts,
    mixed, grads, out,
    taps, ahead, skip, tail, lists, last, last_turned, row_turned,
    feats, gate, glin, gate_prev, glin_next, pad, spill, tiles_f, tiles_b, picked,
    weights, low, edge, edge_out, edge_in, pair, mine, parts, result,
    gate_send, gate_recv, glin_send, glin_recv, near_send, near_recv, share_send, share_recv,
    send0, recv0, send1, recv1, send2, recv2,
):
    me, half = lax.axis_index("ctx"), lax.axis_index("fsdp")
    right, left = lax.rem(me + 1, n), lax.rem(me + n - 1, n)
    blocks, tok = gate.shape[0], gate.shape[1]
    chunks, count = blocks // per, LANES // GROUP
    f32, bf16 = jnp.float32, jnp.bfloat16
    barrier = pltpu.get_barrier_semaphore()

    def greet_share(i, carry):
        pl.semaphore_signal(
            barrier, inc=1, device_id=(me, lax.rem(half + i, m)), device_id_type=MESH
        )
        return carry

    def greet(i, carry):
        pl.semaphore_signal(
            barrier, inc=1, device_id=(lax.rem(me + i, n), half), device_id_type=MESH
        )
        return carry

    lax.fori_loop(1, m, greet_share, 0)
    lax.fori_loop(1, n, greet, 0)
    pl.semaphore_wait(barrier, m + n - 2)

    def started(make, stop, first=1):
        def run(i, carry):
            make(i).start()
            return carry
        lax.fori_loop(first, stop, run, 0)

    def waited(make, stop, first=1):
        def run(i, carry):
            make(i).wait()
            return carry
        lax.fori_loop(first, stop, run, 0)

    def near(j, src, dst, to):
        return pltpu.make_async_remote_copy(
            src_ref=src, dst_ref=dst, send_sem=near_send.at[j], recv_sem=near_recv.at[j],
            device_id=(to, half), device_id_type=MESH,
        )

    entry = [
        near(0, proj.at[tok - 16 : tok], tail, right),
        near(1, starts, lists.at[0], right),
        near(2, starts, lists.at[2], left),
    ]
    for copy in entry:
        copy.start()
    width, skips, groups = taps_own.shape[1], skip_own.shape[1], filt_own.shape[0]
    taps_at = pl.ds(pl.multiple_of(half * width, LANES), width)
    skip_at = pl.ds(pl.multiple_of(half * skips, LANES), skips)
    filt_at = pl.ds(pl.multiple_of(half * groups, 8), groups)

    def shares(j):
        src, dst = (
            (taps_own, taps.at[:, taps_at]),
            (filt_own, ahead.at[filt_at]),
            (skip_own, skip.at[:, skip_at]),
        )[j]

        def make(i):
            return pltpu.make_async_remote_copy(
                src_ref=src, dst_ref=dst, send_sem=share_send.at[j, i],
                recv_sem=share_recv.at[j, i], device_id=(me, lax.rem(half + i, m)),
                device_id_type=MESH,
            )
        return make

    for j in range(3):
        started(shares(j), m)
    lists[1] = starts[...]
    taps[:, taps_at] = taps_own[...]
    ahead[filt_at] = filt_own[...]
    skip[:, skip_at] = skip_own[...]
    weights[...] = jnp.zeros(weights.shape, f32)
    rows = lax.broadcasted_iota(jnp.int32, (tok, LANES), 0)
    cols = lax.broadcasted_iota(jnp.int32, (tok, LANES), 1)
    for copy in entry:
        copy.wait()

    def latest(places):
        best = jnp.full((tok, LANES), -FAR, jnp.int32)
        for j in range(3):
            listed = lists[j, 0:1, :]
            placed = jnp.where(listed < tok, listed + (j - 1) * tok, -FAR)
            best = jnp.maximum(best, jnp.where(placed <= places, placed, -FAR))
        top = jnp.max(best.astype(f32), axis=1, keepdims=True)
        return jnp.broadcast_to(top, (tok, LANES))

    def as_row(column):
        row = jnp.sum(jnp.where(rows == cols, column, 0.0), axis=0, keepdims=True)
        return jnp.broadcast_to(row.astype(jnp.int32), (8, tok))

    turned_last = latest(tok - 1 - rows)
    last[...] = latest(rows).astype(jnp.int32)
    last_turned[...] = turned_last.astype(jnp.int32)
    later = as_row(latest(2 * tok - 1 - rows))
    row_turned[:, :tok] = jnp.where(me < n - 1, later, FAR)
    row_turned[:, tok:] = as_row(turned_last)
    for j in range(3):
        waited(shares(j), m)
    spill[:, 0:8, :] = jnp.zeros((SHORT, 8, LANES), f32)
    spill[:, tok + 8 :, :] = jnp.zeros((SHORT, 8, LANES), f32)

    def lanes(block, part=0):
        return pl.ds(pl.multiple_of((part * blocks + block) * LANES, LANES), LANES)

    def copies(chunk):
        at = pl.ds(chunk * per, per)
        return (
            pltpu.make_async_remote_copy(
                src_ref=gate.at[at], dst_ref=gate_prev.at[at], send_sem=gate_send.at[chunk],
                recv_sem=gate_recv.at[chunk], device_id=(right, half), device_id_type=MESH,
            ),
            pltpu.make_async_remote_copy(
                src_ref=glin.at[at], dst_ref=glin_next.at[at], send_sem=glin_send.at[chunk],
                recv_sem=glin_recv.at[chunk], device_id=(left, half), device_id_type=MESH,
            ),
        )

    def load_rows(block):
        for part in range(3):
            at = lanes(block, part)
            pad[part, 0:8, :] = tail[:, at].astype(f32)[8:16]
            pad[part, 8:, :] = proj[:, at].astype(f32)

    def earlier(part, offset):
        return pad[part, 8 - offset : 8 - offset + tok, :]

    def featurize(block, carry):
        load_rows(block)
        made = []
        for part in range(3):
            at = lanes(block, part)
            total = jnp.zeros((tok, LANES), f32)
            for offset in range(SHORT):
                kept = jnp.where(last[...] <= rows - offset, earlier(part, offset), 0.0)
                total = total + taps[offset : offset + 1, at] * kept
            feats[part, block] = total
            made.append(total)
        gate[block] = (made[1] * made[2]).astype(bf16)
        through = (up[:, lanes(block)].astype(f32) * made[0]).astype(bf16)
        turned = jnp.dot(exchange_matrix(tok), through, preferred_element_type=f32)
        glin[block] = turned.astype(bf16)
        return carry

    def prepare(chunk, carry):
        lax.fori_loop(chunk * per, (chunk + 1) * per, featurize, 0)
        for copy in copies(chunk):
            copy.start()
        return carry

    lax.fori_loop(0, chunks, prepare, 0)

    kept_blocks = blocks // m

    def convolve(block, carry):
        at = lanes(block)
        lag_half, lag_at = block // kept_blocks, 3 * kept_blocks + lax.rem(block, kept_blocks)
        start = last[...]
        start_turned = last_turned[...]
        below = cols <= rows
        fwd_prev = jnp.logical_and(cols > rows, start <= cols - tok)
        fwd_own = jnp.logical_and(below, start <= cols)
        turned = tok - 1 - rows
        bwd_next = jnp.logical_and(cols > rows, row_turned[0:1, :tok] <= turned)
        bwd_own = jnp.logical_and(below, row_turned[0:1, tok:] <= turned)
        lag_prev = jnp.logical_and(cols > turned, start_turned <= cols - tok)
        lag_own = jnp.logical_and(cols <= turned, start_turned <= cols)
        lane = cols // GROUP
        own_gate, own_glin = gate[block], glin[block]
        gate_win = jnp.concatenate([gate_prev[block], own_gate], axis=0)
        glin_win = jnp.concatenate([glin_next[block], own_glin], axis=0)
        glin_f = own_glin.astype(f32)
        filters = ahead[pl.ds(pl.multiple_of(block * count, count), count), :]
        for g in range(count):
            part = slice(g * tok, (g + 1) * tok)
            tile = jnp.broadcast_to(filters[g : g + 1, :], (tok, LEN))
            tile = pltpu.roll(tile, 1, 1, stride=1, stride_axis=0)
            tiles_f[part, :tok] = jnp.where(fwd_prev, tile, 0.0).astype(bf16)
            tiles_f[part, tok:] = jnp.where(fwd_own, tile, 0.0).astype(bf16)
            tiles_b[part, :tok] = jnp.where(bwd_next, tile, 0.0).astype(bf16)
            tiles_b[part, tok:] = jnp.where(bwd_own, tile, 0.0).astype(bf16)
            picked[part, :] = jnp.where(lane == g, glin_f, 0.0).astype(bf16)
        out_f = jnp.dot(tiles_f[...], gate_win, preferred_element_type=f32)
        out_b = jnp.dot(tiles_b[...], glin_win, preferred_element_type=f32)
        product = lax.dot_general(
            picked[...], gate_win, (((1,), (1,)), ((), ())), preferred_element_type=f32
        )
        long_out, spread = out_f[:tok], out_b[:tok]
        for g in range(count):
            part = slice(g * tok, (g + 1) * tok)
            if g:
                long_out = jnp.where(lane == g, out_f[part], long_out)
                spread = jnp.where(lane == g, out_b[part], spread)
            folded = jnp.where(lag_prev, product[part, :tok], 0.0)
            folded = jnp.where(lag_own, product[part, tok:], folded)
            folded = pltpu.roll(folded, 0, 1, stride=1, stride_axis=0)
            weights[lag_half, lag_at, g : g + 1, :] = jnp.sum(folded, axis=0, keepdims=True)
        flip = exchange_matrix(tok)
        high = spread.astype(bf16)
        rest = (spread - high.astype(f32)).astype(bf16)
        spread = jnp.dot(flip, high, preferred_element_type=f32) + jnp.dot(
            flip, rest, preferred_element_type=f32
        )
        gate_f = own_gate.astype(f32)
        query, key, value = feats[0, block], feats[1, block], feats[2, block]
        upstream = up[:, at].astype(f32)
        factor = skip[:, at]
        combined = long_out + factor * gate_f
        mixed[:, at] = (query * combined).astype(bf16)
        through = upstream * query
        weights[lag_half, lax.rem(block, kept_blocks), SHORT : SHORT + 1, :] = jnp.sum(
            through * gate_f, axis=0, keepdims=True
        )
        grad_gate = spread + factor * through
        load_rows(block)
        for part, grad in enumerate((upstream * combined, grad_gate * value, grad_gate * key)):
            at = lanes(block, part)
            column = part * blocks + block
            owner, place = column // (3 * kept_blocks), lax.rem(column, 3 * kept_blocks)
            for offset in range(SHORT):
                kept = jnp.where(start <= rows - offset, grad, 0.0)
                weights[owner, place, offset : offset + 1, :] = jnp.sum(
                    kept * earlier(part, offset), axis=0, keepdims=True
                )
                spill[offset, 8 : tok + 8, :] = taps[offset : offset + 1, at] * kept
            total = spill[0, 0 : tok + 8, :]
            for offset in range(1, SHORT):
                total = total + spill[offset, offset : offset + tok + 8, :]
            grads[:, at] = total[8:].astype(bf16)
            low[column] = total[tok - 8 :]
            edge[column] = total[:8]
        return carry

    def use(chunk, carry):
        for copy in copies(chunk):
            copy.wait_recv()
        lax.fori_loop(chunk * per, (chunk + 1) * per, convolve, 0)
        return carry

    lax.fori_loop(0, chunks, use, 0)

    def sent(chunk, carry):
        for copy in copies(chunk):
            copy.wait_send()
        return carry

    lax.fori_loop(0, chunks, sent, 0)
    edge_out[...] = edge[...].reshape(edge_out.shape).astype(bf16)
    back = near(3, edge_out, edge_in, left)
    back.start()

    def share(i):
        to = lax.rem(half + i, m)
        return pltpu.make_async_remote_copy(
            src_ref=weights.at[to], dst_ref=pair.at[i], send_sem=send0.at[i],
            recv_sem=recv0.at[i], device_id=(me, to), device_id_type=MESH,
        )

    def scatter(i):
        to = lax.rem(me + i, n)
        return pltpu.make_async_remote_copy(
            src_ref=mine.at[to], dst_ref=parts.at[i], send_sem=send1.at[i], recv_sem=recv1.at[i],
            device_id=(to, half), device_id_type=MESH,
        )

    def gather(i):
        return pltpu.make_async_remote_copy(
            src_ref=result.at[me], dst_ref=result.at[me], send_sem=send2.at[i],
            recv_sem=recv2.at[i], device_id=(lax.rem(me + i, n), half), device_id_type=MESH,
        )

    started(share, m)
    waited(share, m)
    owned = lax.fori_loop(1, m, lambda i, total: total + pair[i], weights[half])
    mine[...] = (owned * scaling).reshape(mine.shape).astype(bf16)
    started(scatter, n)
    back.wait()
    edge[...] = edge_in[...].astype(f32).reshape(edge.shape)

    def mend(column, carry):
        at = pl.ds(pl.multiple_of(column * LANES, LANES), LANES)
        total = jnp.concatenate([low[column, :8], low[column, 8:] + edge[column]], axis=0)
        grads[tok - 16 :, at] = total.astype(bf16)
        return carry

    lax.fori_loop(0, 3 * blocks, mend, 0)
    waited(scatter, n)

    def add(i, total):
        return total + parts[i].astype(f32)

    total = lax.fori_loop(1, n, add, mine[me].astype(f32))
    result[me] = total.astype(bf16)
    started(gather, n)
    waited(gather, n)
    out[...] = result[...].astype(f32).reshape(out.shape)


def operate(m, n, scaling, source, upstream, taps, filt, skip, starts):
    tok, channels = upstream.shape
    blocks = channels // LANES
    per = min(4, blocks)
    count = LANES // GROUP
    units = -(-4 * (blocks // m) // n)
    units += units % 2
    f32, bf16, i32 = jnp.float32, jnp.bfloat16, jnp.int32
    vmem = pl.BlockSpec(memory_space=pltpu.VMEM)
    half = pltpu.VMEM((blocks, tok, LANES), bf16)
    tiles = pltpu.VMEM((count * tok, 2 * tok), bf16)
    sems = pltpu.SemaphoreType.DMA((blocks // per,))
    edges = pltpu.VMEM((3 * blocks // 2, 16, LANES), bf16)
    share = pltpu.VMEM((m, n * units, 8, LANES), f32)
    sums = pltpu.VMEM((n, 8 * units, LANES), bf16)
    return pl.pallas_call(
        functools.partial(operator_kernel, m, n, per, scaling),
        in_specs=[vmem] * 6,
        out_specs=[vmem] * 3,
        out_shape=[
            jax.ShapeDtypeStruct((tok, channels), bf16),
            jax.ShapeDtypeStruct((tok, 3 * channels), bf16),
            jax.ShapeDtypeStruct((n * units, 8, LANES), f32),
        ],
        scratch_shapes=[
            pltpu.VMEM((SHORT, 3 * channels), f32),
            pltpu.VMEM((channels // GROUP, LEN), f32),
            pltpu.VMEM((1, channels), f32),
            pltpu.VMEM((16, 3 * channels), bf16),
            pltpu.VMEM((3, 8, LANES), i32),
            pltpu.VMEM((tok, LANES), i32),
            pltpu.VMEM((tok, LANES), i32),
            pltpu.VMEM((8, 2 * tok), i32),
            pltpu.VMEM((3, blocks, tok, LANES), f32),
            half,
            half,
            half,
            half,
            pltpu.VMEM((3, tok + 8, LANES), f32),
            pltpu.VMEM((SHORT, tok + 16, LANES), f32),
            tiles,
            tiles,
            pltpu.VMEM((count * tok, LANES), bf16),
            share,
            pltpu.VMEM((3 * blocks, 16, LANES), f32),
            pltpu.VMEM((3 * blocks, 8, LANES), f32),
            edges,
            edges,
            share,
            sums,
            sums,
            sums,
            sems,
            sems,
            sems,
            sems,
            pltpu.SemaphoreType.DMA((4,)),
            pltpu.SemaphoreType.DMA((4,)),
            pltpu.SemaphoreType.DMA((3, m)),
            pltpu.SemaphoreType.DMA((3, m)),
            pltpu.SemaphoreType.DMA((m,)),
            pltpu.SemaphoreType.DMA((m,)),
            pltpu.SemaphoreType.DMA((n,)),
            pltpu.SemaphoreType.DMA((n,)),
            pltpu.SemaphoreType.DMA((n,)),
            pltpu.SemaphoreType.DMA((n,)),
        ],
        compiler_params=pltpu.CompilerParams(
            collective_id=0, has_side_effects=True, vmem_limit_bytes=50 << 20
        ),
        name="operate",
    )(source, upstream, taps, filt, skip, starts)


def body(proj, short_taps, long_filter, skip, grad_out, starts):
    source, upstream = proj[0], grad_out[0]
    tok, channels = upstream.shape
    count, pairs = lax.axis_size("ctx"), lax.axis_size("fsdp")
    scaling = float(pairs * count * tok) ** (-0.5)
    listed = jnp.pad(starts[0], ((0, 7), (0, LANES - starts.shape[2])), constant_values=tok)
    mixed, grads, sums = operate(
        pairs, count, scaling, source, upstream, short_taps, long_filter[::-1].T, skip[None], listed
    )
    kept = channels // LANES // pairs
    return (
        mixed[None],
        grads[None],
        sums[: 3 * kept, :SHORT].transpose(1, 0, 2).reshape(SHORT, -1),
        sums[3 * kept : 4 * kept].reshape(-1, LEN)[:, ::-1].T,
        sums[:kept, SHORT].reshape(-1),
    )


def solution(mesh):
    window = P("fsdp", "ctx", None)
    return jax.shard_map(
        body,
        mesh=mesh,
        in_specs=(window, P(None, "fsdp"), P(None, "fsdp"), P("fsdp"), window, window),
        out_specs=(window, window, P(None, "fsdp"), P(None, "fsdp"), P("fsdp")),
        check_vma=False,
    )
```

time: 135 us -> 112 us (0.83)
  local copies, waits for them, and re-layouts: 21.9 us -> 11.4 us
  Pallas kernels: 109 us -> 99.4 us
  other arithmetic: 1.69 us -> 0 us
    pallas_call x3 -> x1, Pallas kernels: 109 us -> 99.4 us  [operate(): pl.pallas_call(functools.partial(operator_kernel, m, n, per, scaling), in...]
    unnamed x30 -> x9, local copies, waits for them, and re-layouts: 14.7 us -> 8.58 us
    dynamic_update_slice x1 -> x0, local copies, waits for them, and re-layouts: 2.24 us -> none  [body(): lax.dynamic_update_slice(grads, fixed.astype(jnp.bfloat16), (tok - (SHORT...]
    pallas_call x1 -> x0, other arithmetic: 1.4 us -> none  [operate(): pl.pallas_call(functools.partial(operator_kernel, n, per), in_specs=[vmem...]
    reshape x4 -> x3, local copies, waits for them, and re-layouts: 2.16 us -> 0.78 us  [the longest x1 0.69 us: body(): sums[:3 * kept, :SHORT].transpose(1, 0, 2).reshape(SHORT, -1)]
  transfers between devices with their start and end apart: 1 -> 0, of which waited for: 0 -> 0; matrix products, arithmetic and copies ran while one was open for 4% -> 0% of each run, Pallas kernels for 24% -> 0%
where the time goes in v4:
time: 112 us; the launch traced here: 111 us
  Pallas kernels  99.4 us (89%)
  local copies, waits for them, and re-layouts  11.4 us (10%)
    pallas_call x1, Pallas kernels, operate(): pl.pallas_call(functools.partial(operator_kernel, m, n, per, scaling), in...  99.4 us
    unnamed x9, local copies, waits for them, and re-layouts  8.58 us

profile of v4, /device:TPU:0, one launch (start us, length us, event | category | flops | bytes accessed | tf_op | source)
XLA Modules:
  0.0 111.5 jit_solution(687338760678529518)
XLA Ops:
  0.6 0.7 pad.4.starts
  1.3 0.9 copy.11
  2.2 0.1 rev.6
  2.3 0.0 copy-start
  2.3 1.2 %copy-done = bf16[1,128,4096]{2,1,0:T(8,128)(2,1)S(1)} copy-done((bf16[1,128,4096]{2,1,0:T(8,128)(2,1)S(1)}, bf16[1,128,4096]{2,1,0:T(8,128)(2,1)}, u32[]{:S(2)}) %copy-start) | copy-done | bytes 1048600
  3.5 0.0 copy-start.1
  3.5 0.9 copy-done.1
  4.5 0.0 copy-start.2
  4.5 0.7 copy-done.2
  5.2 99.4 %operate.1 = (bf16[128,4096]{1,0:T(8,128)(2,1)S(1)}, bf16[128,12288]{1,0:T(8,128)(2,1)}, f32[64,8,128]{2,1,0:T(8,128)S(1)}) custom-call(bf16[128,12288]{1,0:T(8,128)(2,1)} %bitcast.19, bf16[128,4096]{1,0:T(8,128)(2,1)S(1)} %bitcast.15, f32[7,6144]{1,0:T(8,128)S(1)} %copy-done.1, f32[128,128]{1,0:T(8,128)S(1)} %bitcast.17, f32[1,2048]{1,0:T(1,128)S(1)} %bitcast.18, ...), custom_call_target="tpu_custom_call" | custom-call | tf_op jit(solution)/shard_map/operate/pallas_call | solution.py:348
  104.6 0.6 slice.11
  105.2 0.7 slice_bitcast_fusion
  105.9 0.1 copy.12
  106.0 0.6 rev.7
  106.7 1.0 copy.15
  107.6 3.8 %copy.16 = bf16[1,128,12288]{2,1,0:T(8,128)(2,1)} copy(bf16[1,128,12288]{2,1,0:T(8,128)(2,1)} %bitcast.20) | data formatting | bytes 6291456
  (1 shorter events, 0.0 us)
Async XLA Ops:
  2.3 1.2 %copy-start = (bf16[1,128,4096]{2,1,0:T(8,128)(2,1)S(1)}, bf16[1,128,4096]{2,1,0:T(8,128)(2,1)}, u32[]{:S(2)}) copy-start(bf16[1,128,4096]{2,1,0:T(8,128)(2,1)} %param.10) | copy-start | bytes 3145732
  3.5 0.9 copy-start.1
  4.5 0.7 copy-start.2

commit v5 on v4

--- a/solution.py
+++ b/solution.py
@@ -131,8 +131,8 @@
     row_turned[:, tok:] = as_row(turned_last)
     for j in range(3):
         waited(shares(j), m)
-    spill[:, 0:8, :] = jnp.zeros((SHORT, 8, LANES), f32)
-    spill[:, tok + 8 :, :] = jnp.zeros((SHORT, 8, LANES), f32)
+    spill[:, :, 0:8, :] = jnp.zeros((2, SHORT, 8, LANES), f32)
+    spill[:, :, tok + 8 :, :] = jnp.zeros((2, SHORT, 8, LANES), f32)
 
     def lanes(block, part=0):
         return pl.ds(pl.multiple_of((part * blocks + block) * LANES, LANES), LANES)
@@ -150,14 +150,14 @@
             ),
         )
 
-    def load_rows(block):
+    def load_rows(block, slot=0):
         for part in range(3):
             at = lanes(block, part)
-            pad[part, 0:8, :] = tail[:, at].astype(f32)[8:16]
-            pad[part, 8:, :] = proj[:, at].astype(f32)
-
-    def earlier(part, offset):
-        return pad[part, 8 - offset : 8 - offset + tok, :]
+            pad[slot, part, 0:8, :] = tail[:, at].astype(f32)[8:16]
+            pad[slot, part, 8:, :] = proj[:, at].astype(f32)
+
+    def earlier(part, offset, slot=0):
+        return pad[slot, part, 8 - offset : 8 - offset + tok, :]
 
     def featurize(block, carry):
         load_rows(block)
@@ -186,7 +186,7 @@
 
     kept_blocks = blocks // m
 
-    def convolve(block, carry):
+    def convolve(block, slot):
         at = lanes(block)
         lag_half, lag_at = block // kept_blocks, 3 * kept_blocks + lax.rem(block, kept_blocks)
         start = last[...]
@@ -209,15 +209,15 @@
             part = slice(g * tok, (g + 1) * tok)
             tile = jnp.broadcast_to(filters[g : g + 1, :], (tok, LEN))
             tile = pltpu.roll(tile, 1, 1, stride=1, stride_axis=0)
-            tiles_f[part, :tok] = jnp.where(fwd_prev, tile, 0.0).astype(bf16)
-            tiles_f[part, tok:] = jnp.where(fwd_own, tile, 0.0).astype(bf16)
-            tiles_b[part, :tok] = jnp.where(bwd_next, tile, 0.0).astype(bf16)
-            tiles_b[part, tok:] = jnp.where(bwd_own, tile, 0.0).astype(bf16)
-            picked[part, :] = jnp.where(lane == g, glin_f, 0.0).astype(bf16)
-        out_f = jnp.dot(tiles_f[...], gate_win, preferred_element_type=f32)
-        out_b = jnp.dot(tiles_b[...], glin_win, preferred_element_type=f32)
+            tiles_f[slot, part, :tok] = jnp.where(fwd_prev, tile, 0.0).astype(bf16)
+            tiles_f[slot, part, tok:] = jnp.where(fwd_own, tile, 0.0).astype(bf16)
+            tiles_b[slot, part, :tok] = jnp.where(bwd_next, tile, 0.0).astype(bf16)
+            tiles_b[slot, part, tok:] = jnp.where(bwd_own, tile, 0.0).astype(bf16)
+            picked[slot, part, :] = jnp.where(lane == g, glin_f, 0.0).astype(bf16)
+        out_f = jnp.dot(tiles_f[slot], gate_win, preferred_element_type=f32)
+        out_b = jnp.dot(tiles_b[slot], glin_win, preferred_element_type=f32)
         product = lax.dot_general(
-            picked[...], gate_win, (((1,), (1,)), ((), ())), preferred_element_type=f32
+            picked[slot], gate_win, (((1,), (1,)), ((), ())), preferred_element_type=f32
         )
         long_out, spread = out_f[:tok], out_b[:tok]
         for g in range(count):
@@ -246,7 +246,7 @@
             through * gate_f, axis=0, keepdims=True
         )
         grad_gate = spread + factor * through
-        load_rows(block)
+        load_rows(block, slot)
         for part, grad in enumerate((upstream * combined, grad_gate * value, grad_gate * key)):
             at = lanes(block, part)
             column = part * blocks + block
@@ -254,21 +254,25 @@
             for offset in range(SHORT):
                 kept = jnp.where(start <= rows - offset, grad, 0.0)
                 weights[owner, place, offset : offset + 1, :] = jnp.sum(
-                    kept * earlier(part, offset), axis=0, keepdims=True
+                    kept * earlier(part, offset, slot), axis=0, keepdims=True
                 )
-                spill[offset, 8 : tok + 8, :] = taps[offset : offset + 1, at] * kept
-            total = spill[0, 0 : tok + 8, :]
+                spill[slot, offset, 8 : tok + 8, :] = taps[offset : offset + 1, at] * kept
+            total = spill[slot, 0, 0 : tok + 8, :]
             for offset in range(1, SHORT):
-                total = total + spill[offset, offset : offset + tok + 8, :]
+                total = total + spill[slot, offset, offset : offset + tok + 8, :]
             grads[:, at] = total[8:].astype(bf16)
             low[column] = total[tok - 8 :]
             edge[column] = total[:8]
+
+    def both(pair_at, carry):
+        convolve(2 * pair_at, 0)
+        convolve(2 * pair_at + 1, 1)
         return carry
 
     def use(chunk, carry):
         for copy in copies(chunk):
             copy.wait_recv()
-        lax.fori_loop(chunk * per, (chunk + 1) * per, convolve, 0)
+        lax.fori_loop(chunk * (per // 2), (chunk + 1) * (per // 2), both, 0)
         return carry
 
     lax.fori_loop(0, chunks, use, 0)
@@ -340,7 +344,7 @@
     f32, bf16, i32 = jnp.float32, jnp.bfloat16, jnp.int32
     vmem = pl.BlockSpec(memory_space=pltpu.VMEM)
     half = pltpu.VMEM((blocks, tok, LANES), bf16)
-    tiles = pltpu.VMEM((count * tok, 2 * tok), bf16)
+    tiles = pltpu.VMEM((2, count * tok, 2 * tok), bf16)
     sems = pltpu.SemaphoreType.DMA((blocks // per,))
     edges = pltpu.VMEM((3 * blocks // 2, 16, LANES), bf16)
     share = pltpu.VMEM((m, n * units, 8, LANES), f32)
@@ -368,11 +372,11 @@
             half,
             half,
             half,
-            pltpu.VMEM((3, tok + 8, LANES), f32),
-            pltpu.VMEM((SHORT, tok + 16, LANES), f32),
+            pltpu.VMEM((2, 3, tok + 8, LANES), f32),
+            pltpu.VMEM((2, SHORT, tok + 16, LANES), f32),
             tiles,
             tiles,
-            pltpu.VMEM((count * tok, LANES), bf16),
+            pltpu.VMEM((2, count * tok, LANES), bf16),
             share,
             pltpu.VMEM((3 * blocks, 16, LANES), f32),
             pltpu.VMEM((3 * blocks, 8, LANES), f32),

time: 112 us -> 109 us (0.973)
  Pallas kernels: 99.4 us -> 97 us
    pallas_call x1, Pallas kernels: 99.4 us -> 97 us  [operate(): pl.pallas_call(functools.partial(operator_kernel, m, n, per, scaling), in...]
where the time goes in v5:
time: 109 us
  Pallas kernels  97 us (89%)
  local copies, waits for them, and re-layouts  11.4 us (10%)
    pallas_call x1, Pallas kernels, operate(): pl.pallas_call(functools.partial(operator_kernel, m, n, per, scaling), in...  97 us
    unnamed x9, local copies, waits for them, and re-layouts  8.58 us

profile of v5, /device:TPU:0, one launch (start us, length us, event | category | flops | bytes accessed | tf_op | source)
XLA Modules:
  0.0 109.0 jit_solution(9329296650125407438)
XLA Ops:
  0.6 0.7 pad.4.starts
  1.3 0.9 copy.11
  2.2 0.1 rev.6
  2.3 0.0 copy-start
  2.3 1.2 %copy-done = bf16[1,128,4096]{2,1,0:T(8,128)(2,1)S(1)} copy-done((bf16[1,128,4096]{2,1,0:T(8,128)(2,1)S(1)}, bf16[1,128,4096]{2,1,0:T(8,128)(2,1)}, u32[]{:S(2)}) %copy-start) | copy-done | bytes 1048600
  3.5 0.0 copy-start.1
  3.5 0.9 copy-done.1
  4.5 0.0 copy-start.2
  4.5 0.7 copy-done.2
  5.2 97.0 %operate.1 = (bf16[128,4096]{1,0:T(8,128)(2,1)S(1)}, bf16[128,12288]{1,0:T(8,128)(2,1)}, f32[64,8,128]{2,1,0:T(8,128)S(1)}) custom-call(bf16[128,12288]{1,0:T(8,128)(2,1)} %bitcast.19, bf16[128,4096]{1,0:T(8,128)(2,1)S(1)} %bitcast.15, f32[7,6144]{1,0:T(8,128)S(1)} %copy-done.1, f32[128,128]{1,0:T(8,128)S(1)} %bitcast.17, f32[1,2048]{1,0:T(1,128)S(1)} %bitcast.18, ...), custom_call_target="tpu_custom_call" | custom-call | tf_op jit(solution)/shard_map/operate/pallas_call | solution.py:352
  102.1 0.6 slice.11
  102.8 0.7 slice_bitcast_fusion
  103.5 0.1 copy.12
  103.5 0.6 rev.7
  104.2 1.0 copy.15
  105.2 3.8 %copy.16 = bf16[1,128,12288]{2,1,0:T(8,128)(2,1)} copy(bf16[1,128,12288]{2,1,0:T(8,128)(2,1)} %bitcast.20) | data formatting | bytes 6291456
  (1 shorter events, 0.0 us)
Async XLA Ops:
  2.3 1.2 %copy-start = (bf16[1,128,4096]{2,1,0:T(8,128)(2,1)S(1)}, bf16[1,128,4096]{2,1,0:T(8,128)(2,1)}, u32[]{:S(2)}) copy-start(bf16[1,128,4096]{2,1,0:T(8,128)(2,1)} %param.10) | copy-start | bytes 3145732
  3.5 0.9 copy-start.1
  4.5 0.7 copy-start.2
